TPU v7x, 128 devices: a whole 4x4x4 slice. The times are simulated.
128 devices in a mesh: site: 8 (over x_hi, z), dom: 16 (over y, x_lo, core).
Axes of the slice: x: 4 (x_hi: 2, x_lo: 2; x = x_hi * 2 + x_lo), y: 4, z: 4, core: 2. Of those that a mesh axis runs over, the one named last changes fastest.
Arguments:
- fields: float32 [9, 128, 128, 256], P(None, 'dom', 'site'), may hold values from -6 to 6
- material: float32 [3, 128, 128, 256], P(None, 'dom', 'site'), may hold values from 0.3 to 1
- send_cell: int32 [8, 16, 16, 128], P('site', 'dom'), may hold values from -1 to 32767, as said below
- recv_node: int32 [8, 16, 16, 128], P('site', 'dom'), may hold values from -1 to 4095, as said below
- elements: int32 [8, 16, 8, 2048], P('site', 'dom'), may hold values from -1 to 4095, as said below
- modulus: float32 [8, 16, 2048], P('site', 'dom'), may hold values from 0.1 to 1
- node_mass: float32 [8, 16, 4096], P('site', 'dom'), may hold values from 0.5 to 2
- outer_flag: int32 [8, 16, 4096], P('site', 'dom'), may hold values 0 or 1
- shared_slot: int32 [8, 16, 4096], P('site', 'dom'), may hold values from -1 to 511, as said below
- stiffness: float32 [24, 24], replicated, as said below
- disp_now: float32 [8, 16, 3, 4096], P('site', 'dom'), may hold values from -0.1 to 0.1
- disp_prev: float32 [8, 16, 3, 4096], P('site', 'dom'), may hold values from -0.1 to 0.1
Outputs:
- basin_out: float32 [9, 128, 128, 256], P(None, 'dom', 'site')
- site_disp: float32 [8, 16, 3, 4096], P('site', 'dom')
Inputs may be any that keep to these rules, and one draw needn't show every extreme that they name: `send_cell`: entry [s, p, q, c] is a cell of slab (s, p), to send to partition q of site model s, or -1. It is live exactly where recv_node[s, q, p, c] is live; live entries come first along c. For each site model the sending slabs are a run of max(half of 16, 1) consecutive slab indices (wrapping); each of their pairs has between half of 128 and 128 live entries, and the first slab of the run fills all 128 to every partition. `recv_node`: entry [s, q, p, c] is the node of partition q of site model s that takes slot c from slab (s, p), or -1; the live nodes of one partition are distinct. `elements`: columns are element slots; a padding slot has -1 in all eight rows and padding slots come last. Each partition has between half of 2048 and 2048 live slots, and in every site model one partition has all 2048. Live entries name nodes of the partition. `shared_slot`: each slot 0 to 511 names exactly one node of a partition; slots below 256 are shared with the previous partition of the site model, the others with the next one (wrapping); other nodes hold -1. `stiffness`: Symmetric.
All inputs are finite; a program needn't handle non-finite values. No bound on the sum of `outer_flag` on one device may be relied on, other than what follows from the above.
Results may differ from a plain program's by a relative error of at most 0.0003.
Values sent between devices are 32-bit elements; how exact they have to be, the bound alone decides.
A program may use at most 128 MiB of HBM per device.

v0:
```python
import jax
import jax.numpy as jnp
from jax import lax
from jax.sharding import PartitionSpec as P

STEPS = 3
NODES_DEV = 4096
SHARE = 256


C_NEAR = 9.0 / 8.0
C_FAR = 1.0 / 24.0
DT_BASIN = 0.25
DT_SITE2 = 0.15


def padded_2(cells, sides, width, closed):
    for axis, dim in sides:
        count = lax.axis_size(axis)
        ends = count if closed else count - 1
        head = lax.slice_in_dim(cells, 0, width, axis=dim)
        tail = lax.slice_in_dim(cells, cells.shape[dim] - width, cells.shape[dim], axis=dim)
        cells = jnp.concatenate(
            [
                lax.ppermute(tail, axis, [(i, (i + 1) % count) for i in range(ends)]),
                cells,
                lax.ppermute(head, axis, [((i + 1) % count, i) for i in range(ends)]),
            ],
            axis=dim,
        )
    return cells


def forward_diff(padded, along, length):

    def window(offset):
        return lax.slice_in_dim(padded, offset, offset + length, axis=along)

    return C_NEAR * (window(3) - window(2)) - C_FAR * (window(4) - window(1))


def backward_diff(padded, along, length):

    def window(offset):
        return lax.slice_in_dim(padded, offset, offset + length, axis=along)

    return C_NEAR * (window(2) - window(1)) - C_FAR * (window(3) - window(0))


def pad_along(field, along):
    widths = [(0, 0)] * field.ndim
    widths[along] = (2, 2)
    return jnp.pad(field, widths)


def velocity_update(velocity, stress, material):
    size_x, size_y, size_z = (velocity.shape[1], velocity.shape[2], velocity.shape[3])
    wide = padded_2(stress, (("site", 2), ("dom", 1)), 2, False)
    stress_xx_x, stress_xy_x, stress_xz_x = (wide[0, :, 2:-2], wide[3, :, 2:-2], wide[4, :, 2:-2])
    stress_xy_y, stress_yy_y, stress_yz_y = (wide[3, 2:-2], wide[1, 2:-2], wide[5, 2:-2])
    buoyancy = material[0]
    vel_x = velocity[0] + DT_BASIN * buoyancy * (
        forward_diff(stress_xx_x, 0, size_x)
        + backward_diff(stress_xy_y, 1, size_y)
        + backward_diff(pad_along(stress[4], 2), 2, size_z)
    )
    vel_y = velocity[1] + DT_BASIN * buoyancy * (
        backward_diff(stress_xy_x, 0, size_x)
        + forward_diff(stress_yy_y, 1, size_y)
        + backward_diff(pad_along(stress[5], 2), 2, size_z)
    )
    vel_z = velocity[2] + DT_BASIN * buoyancy * (
        backward_diff(stress_xz_x, 0, size_x)
        + backward_diff(stress_yz_y, 1, size_y)
        + forward_diff(pad_along(stress[2], 2), 2, size_z)
    )
    return jnp.stack([vel_x, vel_y, vel_z])


def stress_update(velocity, stress, material):
    size_x, size_y, size_z = (velocity.shape[1], velocity.shape[2], velocity.shape[3])
    wide = padded_2(velocity, (("site", 2), ("dom", 1)), 2, False)
    vel_xpad = [wide[0, :, 2:-2], wide[1, :, 2:-2], wide[2, :, 2:-2]]
    vel_ypad = [wide[0, 2:-2], wide[1, 2:-2], wide[2, 2:-2]]
    lame_first, shear_mod = (material[1], material[2])
    strain_xx = backward_diff(vel_xpad[0], 0, size_x)
    strain_yy = backward_diff(vel_ypad[1], 1, size_y)
    strain_zz = backward_diff(pad_along(velocity[2], 2), 2, size_z)
    modulus_p = lame_first + 2.0 * shear_mod
    new_xx = stress[0] + DT_BASIN * (modulus_p * strain_xx + lame_first * (strain_yy + strain_zz))
    new_yy = stress[1] + DT_BASIN * (modulus_p * strain_yy + lame_first * (strain_xx + strain_zz))
    new_zz = stress[2] + DT_BASIN * (modulus_p * strain_zz + lame_first * (strain_xx + strain_yy))
    new_xy = stress[3] + DT_BASIN * shear_mod * (
        forward_diff(vel_ypad[0], 1, size_y) + forward_diff(vel_xpad[1], 0, size_x)
    )
    new_xz = stress[4] + DT_BASIN * shear_mod * (
        forward_diff(pad_along(velocity[0], 2), 2, size_z) + forward_diff(vel_xpad[2], 0, size_x)
    )
    new_yz = stress[5] + DT_BASIN * shear_mod * (
        forward_diff(pad_along(velocity[1], 2), 2, size_z) + forward_diff(vel_ypad[2], 1, size_y)
    )
    return jnp.stack([new_xx, new_yy, new_zz, new_xy, new_xz, new_yz])


def basin_step(velocity, stress, material):
    velocity = velocity_update(velocity, stress, material)
    stress = stress_update(velocity, stress, material)
    return (velocity, stress)


def sample_cells(velocity, send_local):
    flat = velocity.reshape(3, -1)
    picked = flat[:, jnp.maximum(send_local, 0)]
    return jnp.where(send_local[None] >= 0, picked, 0.0)


def place_motion(values, nodes):
    target = jnp.where(nodes >= 0, nodes, NODES_DEV).reshape(-1)
    return (
        jnp.zeros((3, NODES_DEV), jnp.float32).at[:, target].set(values.reshape(3, -1), mode="drop")
    )


def slot_nodes(slots):
    target = jnp.where(slots >= 0, slots, 2 * SHARE)
    return (
        jnp.zeros((2 * SHARE,), jnp.int32)
        .at[target]
        .set(jnp.arange(NODES_DEV, dtype=jnp.int32), mode="drop")
    )


def site_forces(displacement, free_field, drm_mask, outer, element_nodes, element_mod, stiffness):
    count = element_nodes.shape[1]
    live = (element_nodes[0] >= 0).astype(jnp.float32)
    safe = jnp.maximum(element_nodes, 0)
    mask_outer = drm_mask * outer
    mask_inner = drm_mask * (1.0 - outer)
    stacked = jnp.stack([displacement, free_field * mask_inner, free_field * mask_outer])
    gathered = stacked[:, :, safe].reshape(3, 24, count)
    gathered = jnp.transpose(gathered, (1, 0, 2)).reshape(24, 3 * count)
    response = jnp.dot(
        stiffness, gathered, precision=lax.Precision.HIGHEST, preferred_element_type=jnp.float32
    ).reshape(24, 3, count)
    outer_rows = jnp.tile(mask_outer[safe], (3, 1))
    inner_rows = jnp.tile(mask_inner[safe], (3, 1))
    force = (
        element_mod
        * live
        * (-response[:, 0] + outer_rows * response[:, 1] - inner_rows * response[:, 2])
    )
    return (
        jnp.zeros((3, NODES_DEV), jnp.float32)
        .at[:, safe.reshape(-1)]
        .add(force.reshape(3, 8 * count))
    )


def on_device(
    fields,
    material,
    send_cell,
    recv_node,
    elements,
    modulus,
    node_mass,
    outer_flag,
    shared_slot,
    stiffness,
    disp_now,
    disp_prev,
):
    velocity, stress = (fields[0:3], fields[3:9])
    send_local = send_cell[0, 0]
    samples = []
    for segment in range(STEPS):
        velocity, stress = basin_step(velocity, stress, material)
        samples.append(sample_cells(velocity, send_local))
    arrived = lax.all_to_all(
        jnp.concatenate(samples, axis=0), "dom", split_axis=1, concat_axis=1, tiled=True
    )
    motions = [arrived[3 * segment : 3 * segment + 3] for segment in range(STEPS)]
    basin_out = jnp.concatenate([velocity, stress], axis=0)
    recv_local = recv_node[0, 0]
    drm_target = jnp.where(recv_local >= 0, recv_local, NODES_DEV).reshape(-1)
    drm_mask = jnp.zeros((NODES_DEV,), jnp.float32).at[drm_target].set(1.0, mode="drop")
    outer = outer_flag[0, 0].astype(jnp.float32)
    slot_node = slot_nodes(shared_slot[0, 0])
    element_nodes = elements[0, 0]
    element_mod = modulus[0, 0]
    masses = node_mass[0, 0]
    displacement = disp_now[0, 0]
    previous = disp_prev[0, 0]
    free_field = jnp.zeros_like(displacement)
    for segment in range(STEPS):
        free_field = free_field + DT_BASIN * place_motion(motions[segment], recv_local)
        force = site_forces(
            displacement, free_field, drm_mask, outer, element_nodes, element_mod, stiffness
        )
        partial_sum = force[:, slot_node]
        rims = padded_2(partial_sum, (("dom", 1),), SHARE, True)
        total = jnp.concatenate(
            [
                partial_sum[:, :SHARE] + rims[:, :SHARE],
                partial_sum[:, SHARE:] + rims[:, 3 * SHARE :],
            ],
            axis=1,
        )
        force = force.at[:, slot_node].set(total)
        following = 2.0 * displacement - previous + DT_SITE2 * force / masses[None, :]
        previous, displacement = (displacement, following)
    return (basin_out, displacement[None, None])


def solution(mesh):
    placed = (
        P(None, "dom", "site", None),
        P(None, "dom", "site", None),
        P("site", "dom", None, None),
        P("site", "dom", None, None),
        P("site", "dom", None, None),
        P("site", "dom", None),
        P("site", "dom", None),
        P("site", "dom", None),
        P("site", "dom", None),
        P(),
        P("site", "dom", None, None),
        P("site", "dom", None, None),
    )
    return jax.shard_map(
        on_device,
        mesh=mesh,
        in_specs=placed,
        out_specs=(P(None, "dom", "site", None), P("site", "dom", None, None)),
        check_vma=False,
    )
```

profile of v0, /device:TPU:97, one launch (start us, length us, event | category | flops | bytes accessed | tf_op | source)
XLA Modules:
  0.0 1430.5 jit_solution(15173836838359257813)
XLA Ops:
  1.9 2.0 collective-permute-start.1
  4.0 6.9 collective-permute-start
  17.8 8.1 scatter_custom_fusion.1
  27.0 4.2 collective-permute-start.3
  34.9 4.9 collective-permute-done.2
  42.8 7.0 collective-permute-start.4
  51.1 2.9 collective-permute-start.6
  56.1 4.4 collective-permute-done.7
  66.5 8.2 collective-permute-start.8
  75.2 15.6 %scatter_custom_fusion.3 = s32[512]{0:T(512)S(1)} fusion(s32[4096]{0:T(1024)} %bitcast.714, s32[4096]{0:T(1024)S(1)} %iota.3, s32[]{:T(128)} %constant.15.clone.1), kind=kCustom, calls=%fused_computation.669 | custom fusion | bytes 2560 | tf_op jit(solution)/shard_map/scatter | solution.py:129
  93.1 2.4 collective-permute-start.10
  96.7 6.1 collective-permute-done.10
  106.0 7.0 collective-permute-start.12
  114.3 160.3 %gather_fusion.5 = f32[16384]{0:T(1024)} fusion(f32[4096]{0:T(1024)S(1)} %get-tuple-element.26, s32[16384]{0:T(1024)S(1)} %copy-done.3), kind=kCustom, calls=%fused_computation.5 | custom fusion | bytes 196608 | tf_op jit(solution)/shard_map/gather | solution.py:146
  274.6 160.0 %gather_fusion.4 = f32[16384]{0:T(1024)} fusion(f32[4096]{0:T(1024)S(1)} %get-tuple-element.136, s32[16384]{0:T(1024)S(1)} %copy-done.3), kind=kCustom, calls=%fused_computation.4 | custom fusion | bytes 196608 | tf_op jit(solution)/shard_map/gather | solution.py:145
  437.7 2.4 collective-permute-start.14
  442.2 4.4 collective-permute-done.15
  454.3 7.0 collective-permute-start.16
  461.6 8.5 copy.160
  470.1 13.4 gather_fusion
  486.6 2.3 collective-permute-start.19
  488.9 2.2 collective-permute-start.18
  491.5 8.5 copy.162
  499.9 13.4 gather_fusion.1
  520.0 7.0 collective-permute-start.20
  527.4 8.5 copy.164
  535.9 13.3 gather_fusion.2
  551.5 7.7 all-to-all-start
  559.3 6.0 all-to-all-done
  566.7 7.3 scatter_custom_fusion
  574.0 2.2 copy.168
  577.6 7.3 scatter_custom_fusion.5
  584.9 2.2 copy.181
  588.5 7.5 scatter_custom_fusion.8
  596.0 2.8 copy.191
  599.6 5.9 copy.171
  605.5 121.9 %gather_fusion.3 = f32[16384,3,3]{2,1,0:T(4,128)} fusion(f32[3,3,4096]{1,0,2:T(4,128)} %copy.171, s32[16384]{0:T(1024)S(1)} %copy-done.3), kind=kCustom, calls=%fused_computation.3 | custom fusion | bytes 1245184 | tf_op jit(solution)/shard_map/gather | solution.py:140
  727.4 18.3 %copy.215 = f32[8,2048,3,3]{1,0,2,3:T(8,128)S(1)} copy(f32[8,2048,3,3]{3,2,1,0:T(4,128)} %bitcast.641) | data formatting | bytes 1179648
  749.1 5.1 copy.174
  754.2 95.1 %scatter_custom_fusion.2 = f32[3,4096]{0,1:T(8,128)} fusion(s32[16384]{0:T(1024)} %bitcast.707, f32[16384,3]{1,0:T(8,128)} %copy.174, f32[]{:T(128)} %constant.13.clone.1), kind=kCustom, calls=%fused_computation.36 | custom fusion | flops 49152 | bytes 49664 | tf_op jit(solution)/shard_map/scatter-add | solution.py:155
  849.2 2.6 gather_fusion.6
  852.0 7.7 collective-permute-start.25
  862.8 4.9 scatter_fusion
  867.7 2.2 copy.178
  870.1 5.9 copy.182
  876.0 121.9 %gather_fusion.7 = f32[16384,3,3]{2,1,0:T(4,128)} fusion(f32[3,3,4096]{1,0,2:T(4,128)} %copy.182, s32[16384]{0:T(1024)S(1)} %copy-done.4), kind=kCustom, calls=%fused_computation.7 | custom fusion | bytes 1245184 | tf_op jit(solution)/shard_map/gather | solution.py:140
  997.9 18.3 %copy.216 = f32[8,2048,3,3]{1,0,2,3:T(8,128)S(1)} copy(f32[8,2048,3,3]{3,2,1,0:T(4,128)} %bitcast.642) | data formatting | bytes 1179648
  1019.6 5.1 copy.185
  1024.7 95.1 %scatter_custom_fusion.6 = f32[3,4096]{0,1:T(8,128)} fusion(s32[16384]{0:T(1024)} %bitcast.708, f32[16384,3]{1,0:T(8,128)} %copy.185, f32[]{:T(128)} %constant.13.clone.1), kind=kCustom, calls=%fused_computation.32 | custom fusion | flops 49152 | bytes 49664 | tf_op jit(solution)/shard_map/scatter-add | solution.py:155
  1119.7 2.6 gather_fusion.8
  1122.5 10.7 collective-permute-start.27
  1134.5 4.7 scatter_fusion.1
  1139.2 2.2 copy.189
  1141.6 5.9 copy.192
  1147.5 121.9 %gather_fusion.9 = f32[16384,3,3]{2,1,0:T(4,128)} fusion(f32[3,3,4096]{1,0,2:T(4,128)} %copy.192, s32[16384]{0:T(1024)S(1)} %copy-done.4), kind=kCustom, calls=%fused_computation.9 | custom fusion | bytes 1245184 | tf_op jit(solution)/shard_map/gather | solution.py:140
  1269.4 18.3 %copy.217 = f32[8,2048,3,3]{1,0,2,3:T(8,128)S(1)} copy(f32[8,2048,3,3]{3,2,1,0:T(4,128)} %bitcast.640) | data formatting | bytes 1179648
  1295.1 5.1 copy.195
  1300.2 95.1 %scatter_custom_fusion.9 = f32[3,4096]{0,1:T(8,128)} fusion(s32[16384]{0:T(1024)} %bitcast.709, f32[16384,3]{1,0:T(8,128)} %copy.195, f32[]{:T(128)} %constant.13.clone.1), kind=kCustom, calls=%fused_computation.28 | custom fusion | flops 49152 | bytes 49664 | tf_op jit(solution)/shard_map/scatter-add | solution.py:155
  1395.3 2.6 gather_fusion.10
  1398.0 12.4 collective-permute-start.29
  1410.5 2.1 collective-permute-start.22
  1412.6 5.1 collective-permute-start.23
  1418.0 4.6 scatter_fusion.2
  1422.6 2.2 copy.199
  (297 shorter events, 89.0 us)
Async XLA Ops:
  0.6 745.1 %copy-start = (f32[24,24]{1,0:T(8,128)S(1)}, f32[24,24]{1,0:T(8,128)}, u32[]{:S(2)}) copy-start(f32[24,24]{1,0:T(8,128)} %param.21) | copy-start | bytes 6916
  0.6 26.0 %copy-start.2 = (f32[9,8,16,256]{3,2,1,0:T(8,128)S(1)}, f32[9,8,16,256]{3,2,1,0:T(8,128)}, u32[]{:S(2)}) copy-start(f32[9,8,16,256]{3,2,1,0:T(8,128)} %param.12) | copy-start | bytes 3538948
  1.9 24.8 %collective-permute-start.1 = (f32[6,8,2,256]{3,2,1,0:T(2,128)S(1)}, f32[6,8,2,256]{3,2,1,0:T(2,128)S(1)}, u32[]{:S(2)}, u32[]{:S(2)}) collective-permute-start(f32[6,8,2,256]{3,2,1,0:T(2,128)S(1)} %get-tuple-element.80), channel_id=1, source_target_pairs={{16,0},{32,16},{48,32},{64,48},{80,64},{96,80},{112,96},{17,1},{33... | collective-permute-start | bytes 294920 | tf_op jit(solution)/shard_map/ppermute | solution.py:27
  4.0 22.8 %collective-permute-start = (f32[6,8,2,256]{3,2,1,0:T(2,128)S(1)}, f32[6,8,2,256]{3,2,1,0:T(2,128)S(1)}, u32[]{:S(2)}, u32[]{:S(2)}) collective-permute-start(f32[6,8,2,256]{3,2,1,0:T(2,128)S(1)} %get-tuple-element.79), channel_id=1, source_target_pairs={{0,16},{16,32},{32,48},{48,64},{64,80},{80,96},{96,112},{1,17},{17... | collective-permute-start | bytes 294920 | tf_op jit(solution)/shard_map/ppermute | solution.py:25
  14.4 12.6 copy-start.43
  15.1 10.8 copy-start.58
  26.7 13.0 copy-start.1
  27.0 7.9 collective-permute-start.3
  31.2 8.5 collective-permute-start.2
  40.1 9.7 copy-start.55
  40.9 8.9 collective-permute-start.5
  42.8 8.1 collective-permute-start.4
  49.8 420.3 %copy-start.52 = (s32[2048]{0:T(1024)}, s32[2048]{0:T(1024)S(1)}, u32[]{:S(2)}) copy-start(s32[2048]{0:T(1024)S(1)} %bitcast_clamp_fusion) | copy-start | bytes 24580
  51.1 5.0 collective-permute-start.6
  54.0 6.5 collective-permute-start.7
  64.6 26.3 %collective-permute-start.9 = (f32[6,8,2,256]{3,2,1,0:T(2,128)S(1)}, f32[6,8,2,256]{3,2,1,0:T(2,128)S(1)}, u32[]{:S(2)}, u32[]{:S(2)}) collective-permute-start(f32[6,8,2,256]{3,2,1,0:T(2,128)S(1)} %get-tuple-element.93), channel_id=1, source_target_pairs={{16,0},{32,16},{48,32},{64,48},{80,64},{96,80},{112,96},{17,1},{33... | collective-permute-start | bytes 294920 | tf_op jit(solution)/shard_map/ppermute | solution.py:27
  66.5 24.4 %collective-permute-start.8 = (f32[6,8,2,256]{3,2,1,0:T(2,128)S(1)}, f32[6,8,2,256]{3,2,1,0:T(2,128)S(1)}, u32[]{:S(2)}, u32[]{:S(2)}) collective-permute-start(f32[6,8,2,256]{3,2,1,0:T(2,128)S(1)} %get-tuple-element.92), channel_id=1, source_target_pairs={{0,16},{16,32},{32,48},{48,64},{64,80},{80,96},{96,112},{1,17},{17... | collective-permute-start | bytes 294920 | tf_op jit(solution)/shard_map/ppermute | solution.py:25
  90.9 12.0 copy-start.17
  91.2 5.6 collective-permute-start.11
  93.1 9.8 collective-permute-start.10
  103.3 10.3 copy-start.40
  103.3 11.0 copy-start.3
  104.1 333.5 %collective-permute-start.13 = (f32[3,8,2,256]{3,2,1,0:T(2,128)S(1)}, f32[3,8,2,256]{3,2,1,0:T(2,128)S(1)}, u32[]{:S(2)}, u32[]{:S(2)}) collective-permute-start(f32[3,8,2,256]{3,2,1,0:T(2,128)S(1)} %get-tuple-element.112), channel_id=1, source_target_pairs={{16,0},{32,16},{48,32},{64,48},{80,64},{96,80},{112,96},{17,1},{33... | collective-permute-start | bytes 147464 | tf_op jit(solution)/shard_map/ppermute | solution.py:27
  106.0 331.6 %collective-permute-start.12 = (f32[3,8,2,256]{3,2,1,0:T(2,128)S(1)}, f32[3,8,2,256]{3,2,1,0:T(2,128)S(1)}, u32[]{:S(2)}, u32[]{:S(2)}) collective-permute-start(f32[3,8,2,256]{3,2,1,0:T(2,128)S(1)} %get-tuple-element.111), channel_id=1, source_target_pairs={{0,16},{16,32},{32,48},{48,64},{64,80},{80,96},{96,112},{1,17},{17... | collective-permute-start | bytes 147464 | tf_op jit(solution)/shard_map/ppermute | solution.py:25
  274.6 160.0 %copy-start.44 = (f32[1,16,8,128]{3,2,1,0:T(8,128)S(1)}, f32[1,16,8,128]{3,2,1,0:T(8,128)}, u32[]{:S(2)}) copy-start(f32[1,16,8,128]{3,2,1,0:T(8,128)} %broadcast_bitcast_fusion) | copy-start | bytes 196612
  437.7 10.7 copy-start.37
  437.7 4.5 collective-permute-start.14
  440.2 6.5 collective-permute-start.15
  449.8 11.4 copy-start.33
  449.8 11.4 copy-start.34
  449.8 11.4 copy-start.35
  452.3 33.2 %collective-permute-start.17 = (f32[6,8,2,256]{3,2,1,0:T(2,128)S(1)}, f32[6,8,2,256]{3,2,1,0:T(2,128)S(1)}, u32[]{:S(2)}, u32[]{:S(2)}) collective-permute-start(f32[6,8,2,256]{3,2,1,0:T(2,128)S(1)} %get-tuple-element.91), channel_id=1, source_target_pairs={{16,0},{32,16},{48,32},{64,48},{80,64},{96,80},{112,96},{17,1},{33... | collective-permute-start | bytes 294920 | tf_op jit(solution)/shard_map/ppermute | solution.py:27
  454.3 31.2 %collective-permute-start.16 = (f32[6,8,2,256]{3,2,1,0:T(2,128)S(1)}, f32[6,8,2,256]{3,2,1,0:T(2,128)S(1)}, u32[]{:S(2)}, u32[]{:S(2)}) collective-permute-start(f32[6,8,2,256]{3,2,1,0:T(2,128)S(1)} %get-tuple-element.90), channel_id=1, source_target_pairs={{0,16},{16,32},{32,48},{48,64},{64,80},{80,96},{96,112},{1,17},{17... | collective-permute-start | bytes 294920 | tf_op jit(solution)/shard_map/ppermute | solution.py:25
  486.6 28.5 %collective-permute-start.19 = (f32[6,2,20,256]{3,2,1,0:T(8,128)}, f32[6,2,20,256]{3,2,1,0:T(8,128)S(1)}, u32[]{:S(2)}, u32[]{:S(2)}) collective-permute-start(f32[6,2,20,256]{3,2,1,0:T(8,128)} %get-tuple-element.71), channel_id=1, source_target_pairs={{0,1},{1,2},{2,3},{3,4},{4,5},{5,6},{6,7},{7,8},{8,9},{9,10},{10,1... | collective-permute-start | bytes 737288 | tf_op jit(solution)/shard_map/ppermute | solution.py:25
  488.9 26.2 %collective-permute-start.18 = (f32[6,2,20,256]{3,2,1,0:T(8,128)}, f32[6,2,20,256]{3,2,1,0:T(8,128)S(1)}, u32[]{:S(2)}, u32[]{:S(2)}) collective-permute-start(f32[6,2,20,256]{3,2,1,0:T(8,128)} %get-tuple-element.70), channel_id=1, source_target_pairs={{1,0},{2,1},{3,2},{4,3},{5,4},{6,5},{7,6},{8,7},{9,8},{10,9},{11,1... | collective-permute-start | bytes 737288 | tf_op jit(solution)/shard_map/ppermute | solution.py:27
  491.4 8.5 copy-start.53
  499.9 15.1 %copy-start.5 = (f32[8,16,256]{2,1,0:T(8,128)S(1)}, f32[8,16,256]{2,1,0:T(8,128)}, u32[]{:S(2)}) copy-start(f32[8,16,256]{2,1,0:T(8,128)} %get-tuple-element.42) | copy-start | bytes 393220
  499.9 15.1 %copy-start.7 = (f32[8,16,256]{2,1,0:T(8,128)S(1)}, f32[8,16,256]{2,1,0:T(8,128)}, u32[]{:S(2)}) copy-start(f32[8,16,256]{2,1,0:T(8,128)} %get-tuple-element.50) | copy-start | bytes 393220
  518.1 41.1 %collective-permute-start.21 = (f32[3,8,2,256]{3,2,1,0:T(2,128)S(1)}, f32[3,8,2,256]{3,2,1,0:T(2,128)S(1)}, u32[]{:S(2)}, u32[]{:S(2)}) collective-permute-start(f32[3,8,2,256]{3,2,1,0:T(2,128)S(1)} %get-tuple-element.110), channel_id=1, source_target_pairs={{16,0},{32,16},{48,32},{64,48},{80,64},{96,80},{112,96},{17,1},{33... | collective-permute-start | bytes 147464 | tf_op jit(solution)/shard_map/ppermute | solution.py:27
  520.0 39.1 %collective-permute-start.20 = (f32[3,8,2,256]{3,2,1,0:T(2,128)S(1)}, f32[3,8,2,256]{3,2,1,0:T(2,128)S(1)}, u32[]{:S(2)}, u32[]{:S(2)}) collective-permute-start(f32[3,8,2,256]{3,2,1,0:T(2,128)S(1)} %get-tuple-element.109), channel_id=1, source_target_pairs={{0,16},{16,32},{32,48},{48,64},{64,80},{80,96},{96,112},{1,17},{17... | collective-permute-start | bytes 147464 | tf_op jit(solution)/shard_map/ppermute | solution.py:25
  527.4 23.4 %copy-start.57 = (pred[16,128]{1,0:T(8,128)(4,1)S(1)}, pred[16,128]{1,0:T(8,128)(4,1)}, u32[]{:S(2)}) copy-start(pred[16,128]{1,0:T(8,128)(4,1)} %compare_bitcast_fusion) | copy-start | bytes 6148
  551.5 13.8 all-to-all-start
  559.2 14.8 %copy-start.29 = (f32[3,8,2,256]{3,2,1,0:T(2,128)}, f32[3,8,2,256]{3,2,1,0:T(2,128)S(1)}, u32[]{:S(2)}) copy-start(f32[3,8,2,256]{3,2,1,0:T(2,128)S(1)} %collective-permute-done.21) | copy-start | bytes 147460
  559.2 14.8 %copy-start.31 = (f32[3,8,2,256]{3,2,1,0:T(2,128)}, f32[3,8,2,256]{3,2,1,0:T(2,128)S(1)}, u32[]{:S(2)}) copy-start(f32[3,8,2,256]{3,2,1,0:T(2,128)S(1)} %collective-permute-done.20) | copy-start | bytes 147460
  588.5 11.0 copy-start.46
  754.2 95.1 %copy-start.56 = (s32[1024]{0:T(1024)S(1)}, s32[1024]{0:T(1024)}, u32[]{:S(2)}) copy-start(s32[1024]{0:T(1024)} %pad_clamp_fusion) | copy-start | bytes 12292
  754.2 105.5 %copy-start.45 = (f32[3,4096]{1,0:T(4,128)S(1)}, f32[3,4096]{1,0:T(4,128)}, u32[]{:S(2)}) copy-start(f32[3,4096]{1,0:T(4,128)} %copy.191) | copy-start | bytes 147460
  754.2 105.5 %copy-start.50 = (f32[3,4096]{1,0:T(4,128)S(1)}, f32[3,4096]{1,0:T(4,128)}, u32[]{:S(2)}) copy-start(f32[3,4096]{1,0:T(4,128)} %get-tuple-element.24) | copy-start | bytes 147460
  851.9 18.0 %copy-start.41 = (f32[1,1,3,4096]{3,1,2,0:T(1,128)S(1)}, f32[1,1,3,4096]{3,1,2,0:T(1,128)}, u32[]{:S(2)}) copy-start(f32[1,1,3,4096]{3,1,2,0:T(1,128)} %param.22) | copy-start | bytes 147460
  851.9 18.0 %copy-start.51 = (f32[1,1,4096]{2,1,0:T(1,128)S(1)}, f32[1,1,4096]{2,1,0:T(1,128)}, u32[]{:S(2)}) copy-start(f32[1,1,4096]{2,1,0:T(1,128)} %param.18) | copy-start | bytes 49156
  851.9 18.0 %copy-start.54 = (f32[1,1,3,4096]{3,1,2,0:T(1,128)S(1)}, f32[1,1,3,4096]{3,1,2,0:T(1,128)}, u32[]{:S(2)}) copy-start(f32[1,1,3,4096]{3,1,2,0:T(1,128)} %param.23) | copy-start | bytes 147460
  851.9 8.5 collective-permute-start.24
  852.0 10.4 collective-permute-start.25
  859.7 10.4 copy-start.49
  1122.4 11.5 collective-permute-start.26
  1122.5 11.7 collective-permute-start.27
  1133.2 8.3 copy-start.47
  1397.9 19.7 %collective-permute-start.28 = (f32[3,256]{0,1:T(8,128)S(1)}, f32[3,256]{0,1:T(8,128)S(1)}, u32[]{:S(2)}, u32[]{:S(2)}) collective-permute-start(f32[3,256]{0,1:T(8,128)S(1)} %get-tuple-element.117), channel_id=1, source_target_pairs={{0,1},{1,2},{2,3},{3,4},{4,5},{5,6},{6,7},{7,8},{8,9},{9,10},{10,1... | collective-permute-start | bytes 9224 | tf_op jit(solution)/shard_map/ppermute | solution.py:25
  1398.0 19.6 %collective-permute-start.29 = (f32[3,256]{0,1:T(8,128)S(1)}, f32[3,256]{0,1:T(8,128)S(1)}, u32[]{:S(2)}, u32[]{:S(2)}) collective-permute-start(f32[3,256]{0,1:T(8,128)S(1)} %get-tuple-element.118), channel_id=1, source_target_pairs={{1,0},{2,1},{3,2},{4,3},{5,4},{6,5},{7,6},{8,7},{9,8},{10,9},{11,1... | collective-permute-start | bytes 9224 | tf_op jit(solution)/shard_map/ppermute | solution.py:27
  1410.5 15.1 %copy-start.8 = (f32[8,16,256]{2,1,0:T(8,128)S(1)}, f32[8,16,256]{2,1,0:T(8,128)}, u32[]{:S(2)}) copy-start(f32[8,16,256]{2,1,0:T(8,128)} %get-tuple-element.50) | copy-start | bytes 393220
  1410.5 15.1 %copy-start.30 = (f32[3,8,2,256]{3,2,1,0:T(2,128)S(1)}, f32[3,8,2,256]{3,2,1,0:T(2,128)}, u32[]{:S(2)}) copy-start(f32[3,8,2,256]{3,2,1,0:T(2,128)} %copy-done.29) | copy-start | bytes 147460
  1410.5 15.1 %copy-start.32 = (f32[3,8,2,256]{3,2,1,0:T(2,128)S(1)}, f32[3,8,2,256]{3,2,1,0:T(2,128)}, u32[]{:S(2)}) copy-start(f32[3,8,2,256]{3,2,1,0:T(2,128)} %copy-done.31) | copy-start | bytes 147460
  1410.5 15.1 %collective-permute-start.22 = (f32[3,2,20,256]{3,2,1,0:T(8,128)S(1)}, f32[3,2,20,256]{3,2,1,0:T(8,128)S(1)}, u32[]{:S(2)}, u32[]{:S(2)}) collective-permute-start(f32[3,2,20,256]{3,2,1,0:T(8,128)S(1)} %get-tuple-element.98), channel_id=1, source_target_pairs={{0,1},{1,2},{2,3},{3,4},{4,5},{5,6},{6,7},{7,8},{8,9},{9,10},{10,1... | collective-permute-start | bytes 368648 | tf_op jit(solution)/shard_map/ppermute | solution.py:25
  1412.6 13.0 collective-permute-start.23
  (26 other events, 95.7 us)
where the time goes:
time: 1440 us; the launch traced here: 1430 us
  local copies, waits for them, and re-layouts  949 us (66%)
  other arithmetic  320 us (22%)
  starting transfers between devices  125 us (9%)
  waiting for transfers between devices  32.1 us (2%)
    gather x3, local copies, waits for them, and re-layouts, site_forces(): gathered = stacked[:, :, safe].reshape(3, 24, count)  366 us
    scatter-add x3, other arithmetic, site_forces(): return jnp.zeros((3, NODES_DEV), jnp.float32).at[:, safe.reshape(-1)].add...  285 us
    gather x1, local copies, waits for them, and re-layouts, site_forces(): inner_rows = jnp.tile(mask_inner[safe], (3, 1))  160 us
    gather x1, local copies, waits for them, and re-layouts, site_forces(): outer_rows = jnp.tile(mask_outer[safe], (3, 1))  160 us
    ppermute x15, starting transfers between devices, padded_2(): lax.ppermute(tail, axis, [(i, (i + 1) % count) for i in range(ends)])  59 us
    unnamed x125, local copies, waits for them, and re-layouts  58.2 us
    ppermute x15, starting transfers between devices, padded_2(): lax.ppermute(head, axis, [((i + 1) % count, i) for i in range(ends)])  58 us
    gather x6, local copies, waits for them, and re-layouts, sample_cells(): picked = flat[:, jnp.maximum(send_local, 0)]  44.8 us
  transfers between devices with their start and end apart: 31, of which 13 were waited for; matrix products, arithmetic and copies ran while one was open for 31% of the time, Pallas kernels for 0%

commit v1 on v0

v1 whole, which is shorter than its diff:
```python
import functools

import jax
import jax.numpy as jnp
from jax import lax
from jax.experimental import pallas as pl
from jax.experimental.pallas import tpu as pltpu
from jax.sharding import PartitionSpec as P

STEPS = 3
SHARE = 256
C_NEAR = 9.0 / 8.0
C_FAR = 1.0 / 24.0
DT = 0.25
DT_SITE2 = 0.15
MESH = pl.DeviceIdType.MESH
LANES = 128
COLS = 256
F32 = jnp.float32
BF16 = jnp.bfloat16
NT = (((1,), (1,)), ((), ()))

STRESS_X = ((3, "F"), (6, "B"), (7, "B"))
STRESS_Y = ((6, "B"), (4, "F"), (8, "B"))
VEL_X = ((0, "B"), (1, "F"), (2, "F"))
VEL_Y = ((0, "F"), (1, "B"), (2, "F"))
LOW = {"B": 2, "F": 1}
HIGH = {"B": 1, "F": 2}


def take_lanes(table, lanes):
    return lax.gather(
        table,
        lanes[..., None],
        lax.GatherDimensionNumbers(
            offset_dims=(),
            collapsed_slice_dims=(1,),
            start_index_map=(1,),
            operand_batching_dims=(0,),
            start_indices_batching_dims=(0,),
        ),
        (1, 1),
        mode=lax.GatherScatterMode.PROMISE_IN_BOUNDS,
    )


def stencil(kind, m2, m1, f, p1, p2):
    if kind == "B":
        return C_NEAR * (f - m1) - C_FAR * (p1 - m2)
    return C_NEAR * (p1 - f) - C_FAR * (p2 - m1)


def diff_rolled(kind, f, axis, index, low, high):
    n = f.shape[axis]
    below = lambda v, edge: jnp.where(index == 0, edge, pltpu.roll(v, 1, axis))
    above = lambda v, edge: jnp.where(index == n - 1, edge, pltpu.roll(v, n - 1, axis))
    m1 = below(f, low[-1])
    p1 = above(f, high[0])
    if kind == "B":
        return stencil(kind, below(m1, low[0]), m1, f, p1, None)
    return stencil(kind, None, m1, f, p1, above(p1, high[1]))


def split(v):
    top = v.astype(BF16).astype(F32)
    return top, v - top


def kernel(
    n_site,
    n_dom,
    fields,
    mat,
    send_cell,
    recv_node,
    elem,
    modulus,
    mass_in,
    flag_in,
    slot_in,
    stiff,
    now_in,
    prev_in,
    basin_out,
    disp_out,
    st,
    y_low,
    y_high,
    y_to_low,
    y_to_high,
    samp_send,
    samp_recv,
    rim_send,
    rim_recv,
    oh_recv,
    oh_elem,
    lhs,
    table,
    inn,
    out,
    cols,
    kblock,
    fe,
    u_now,
    u_prev,
    free,
    code,
    mass,
    slot,
    slot_node,
    force,
    in_sem,
    out_sem,
    x_send_sem,
    x_recv_sem,
    y_send_sem,
    y_recv_sem,
    s_send_sem,
    s_recv_sem,
    r_send_sem,
    r_recv_sem,
):
    cx, cy, nz = mat.shape[1:]
    rows_n = u_now.shape[1]
    n_el = elem.shape[1]
    n_arr = n_dom * LANES
    me_s = lax.axis_index("site")
    me_d = lax.axis_index("dom")

    load = pltpu.make_async_copy(fields, st.at[:, pl.ds(2, cx)], in_sem)
    load.start()
    st[:, pl.ds(0, 2)] = jnp.zeros((9, 2, cy, nz), F32)
    st[:, pl.ds(2 + cx, 2)] = jnp.zeros((9, 2, cy, nz), F32)
    y_low[...] = jnp.zeros(y_low.shape, F32)
    y_high[...] = jnp.zeros(y_high.shape, F32)

    barrier = pltpu.get_barrier_semaphore()

    def greet(d, carry):
        pl.semaphore_signal(
            barrier, inc=1, device_id=(me_s, lax.rem(me_d + d, n_dom)), device_id_type=MESH
        )
        return carry

    lax.fori_loop(1, n_dom, greet, 0)
    for step in (-1, 1):
        there = me_s + step

        @pl.when((there >= 0) & (there < n_site))
        def _():
            pl.semaphore_signal(barrier, inc=1, device_id=(there, me_d), device_id_type=MESH)

    load.wait()

    row_iota = lax.broadcasted_iota(jnp.int32, (cy, nz), 0)
    lane_iota = lax.broadcasted_iota(jnp.int32, (cy, nz), 1)

    def x_copies(which, fields_x, upward):
        made = []
        for at, (f, kind) in enumerate(fields_x):
            if upward:
                width = LOW[kind]
                src = st.at[f, pl.ds(2 + cx - width, width)]
                dst = st.at[f, pl.ds(2 - width, width)]
                there = me_d + 1
            else:
                width = HIGH[kind]
                src = st.at[f, pl.ds(2, width)]
                dst = st.at[f, pl.ds(2 + cx, width)]
                there = me_d - 1
            sem = (which, 1 if upward else 0, at)
            made.append(
                pltpu.make_async_remote_copy(
                    src_ref=src,
                    dst_ref=dst,
                    send_sem=x_send_sem.at[sem],
                    recv_sem=x_recv_sem.at[sem],
                    device_id=(me_s, there),
                    device_id_type=MESH,
                )
            )
        return made

    def y_copy(which, fields_y, upward):
        count = sum((LOW if upward else HIGH)[kind] for _, kind in fields_y)
        src, dst = (y_to_high, y_low) if upward else (y_to_low, y_high)
        sem = (which, 1 if upward else 0)
        return pltpu.make_async_remote_copy(
            src_ref=src.at[which, pl.ds(0, count)],
            dst_ref=dst.at[which, pl.ds(0, count)],
            send_sem=y_send_sem.at[sem],
            recv_sem=y_recv_sem.at[sem],
            device_id=(me_s + (1 if upward else -1), me_d),
            device_id_type=MESH,
        )

    has = {
        "x": (me_d > 0, me_d < n_dom - 1),
        "y": (me_s > 0, me_s < n_site - 1),
    }

    def halo_start(which, fields_x, fields_y):
        for upward in (False, True):

            @pl.when(has["x"][upward])
            def _():
                for copy in x_copies(which, fields_x, upward):
                    copy.start()

            @pl.when(has["y"][upward])
            def _():
                y_copy(which, fields_y, upward).start()

    def halo_wait(which, fields_x, fields_y):
        for upward in (False, True):

            @pl.when(has["x"][upward])
            def _():
                for copy in x_copies(which, fields_x, upward):
                    copy.wait_send()

            @pl.when(has["x"][not upward])
            def _():
                for copy in x_copies(which, fields_x, upward):
                    copy.wait_recv()

            @pl.when(has["y"][upward])
            def _():
                y_copy(which, fields_y, upward).wait_send()

            @pl.when(has["y"][not upward])
            def _():
                y_copy(which, fields_y, upward).wait_recv()

    def y_pack(which, fields_y, x, planes):
        at = 0
        for f, kind in fields_y:
            for k in range(LOW[kind]):
                y = cy - LOW[kind] + k
                y_to_high[which, at, pl.ds(x, 1), :] = planes[f][y : y + 1]
                at += 1
        at = 0
        for f, kind in fields_y:
            for k in range(HIGH[kind]):
                y_to_low[which, at, pl.ds(x, 1), :] = planes[f][k : k + 1]
                at += 1

    def y_edges(which, fields_y, x):
        edges = {}
        low_at = high_at = 0
        for f, kind in fields_y:
            low = [y_low[which, low_at + k, pl.ds(x, 1), :] for k in range(LOW[kind])]
            high = [y_high[which, high_at + k, pl.ds(x, 1), :] for k in range(HIGH[kind])]
            low_at += LOW[kind]
            high_at += HIGH[kind]
            edges[f] = (low, high)
        return edges

    def diff_x(kind, f, x):
        at = lambda o: st[f, x + 2 + o]
        if kind == "B":
            return stencil(kind, at(-2), at(-1), at(0), at(1), None)
        return stencil(kind, None, at(-1), at(0), at(1), at(2))

    def diff_y(kind, f, x, edges):
        low, high = edges[f]
        return diff_rolled(kind, st[f, x + 2], 0, row_iota, low, high)

    def diff_z(kind, f, x):
        return diff_rolled(kind, st[f, x + 2], 1, lane_iota, (0.0, 0.0), (0.0, 0.0))

    def velocity_half():
        def body(x, carry):
            edges = y_edges(0, STRESS_Y, x)
            b = DT * mat[0, x]
            planes = {
                0: st[0, x + 2]
                + b * (diff_x("F", 3, x) + diff_y("B", 6, x, edges) + diff_z("B", 7, x)),
                1: st[1, x + 2]
                + b * (diff_x("B", 6, x) + diff_y("F", 4, x, edges) + diff_z("B", 8, x)),
                2: st[2, x + 2]
                + b * (diff_x("B", 7, x) + diff_y("B", 8, x, edges) + diff_z("F", 5, x)),
            }
            for f, plane in planes.items():
                st[f, x + 2] = plane
            y_pack(1, VEL_Y, x, planes)
            return carry

        lax.fori_loop(0, cx, body, 0)

    def stress_half():
        def body(x, carry):
            edges = y_edges(1, VEL_Y, x)
            lam, mu = mat[1, x], mat[2, x]
            exx = diff_x("B", 0, x)
            eyy = diff_y("B", 1, x, edges)
            ezz = diff_z("B", 2, x)
            wide = lam + 2.0 * mu
            shear = DT * mu
            planes = {
                3: st[3, x + 2] + DT * (wide * exx + lam * (eyy + ezz)),
                4: st[4, x + 2] + DT * (wide * eyy + lam * (exx + ezz)),
                5: st[5, x + 2] + DT * (wide * ezz + lam * (exx + eyy)),
                6: st[6, x + 2] + shear * (diff_y("F", 0, x, edges) + diff_x("F", 1, x)),
                7: st[7, x + 2] + shear * (diff_z("F", 0, x) + diff_x("F", 2, x)),
                8: st[8, x + 2] + shear * (diff_z("F", 1, x) + diff_y("F", 2, x, edges)),
            }
            for f, plane in planes.items():
                st[f, x + 2] = plane
            y_pack(0, STRESS_Y, x, planes)
            return carry

        lax.fori_loop(0, cx, body, 0)

    def sample(k):
        cell = send_cell[...]
        low, high = cell & (LANES - 1), cell >> 7
        halves = nz // LANES

        def body(x, acc):
            acc = list(acc)
            for y in range(cy):
                for half in range(halves):
                    here = high == (x * cy + y) * halves + half
                    for c in range(3):
                        row = st[c, x + 2, y : y + 1, half * LANES : (half + 1) * LANES]
                        got = take_lanes(jnp.broadcast_to(row, cell.shape), low)
                        acc[c] = jnp.where(here, got, acc[c])
            return tuple(acc)

        acc = lax.fori_loop(0, cx, body, (jnp.zeros(cell.shape, F32),) * 3)
        for c in range(3):
            for q in range(n_dom):
                samp_send[k, q, c : c + 1, :] = acc[c][q : q + 1]

    def sample_copy(k, d):
        there = lax.rem(me_d + d, n_dom)
        return pltpu.make_async_remote_copy(
            src_ref=samp_send.at[k, there],
            dst_ref=samp_recv.at[k, me_d],
            send_sem=s_send_sem.at[k, d],
            recv_sem=s_recv_sem.at[k, d],
            device_id=(me_s, there),
            device_id_type=MESH,
        )

    def sample_start(k):
        def body(d, carry):
            sample_copy(k, d).start()
            return carry

        lax.fori_loop(1, n_dom, body, 0)
        samp_recv[k, me_d] = samp_send[k, me_d]

    def sample_wait(k):
        def body(d, carry):
            here = lax.rem(me_d + n_dom - d, n_dom)
            copy = pltpu.make_async_remote_copy(
                src_ref=samp_send.at[k, here],
                dst_ref=samp_recv.at[k, here],
                send_sem=s_send_sem.at[k, d],
                recv_sem=s_recv_sem.at[k, d],
                device_id=(me_s, here),
                device_id_type=MESH,
            )
            copy.wait_recv()
            sample_copy(k, d).wait_send()
            return carry

        lax.fori_loop(1, n_dom, body, 0)

    high_iota = lax.broadcasted_iota(jnp.int32, (rows_n, LANES), 0)

    def build_table(values, group):
        for h in range(rows_n):
            for half in range(COLS // LANES):
                row = values[h : h + 1, half * LANES : (half + 1) * LANES]
                table[group, h * (COLS // LANES) + half] = jnp.broadcast_to(row, (8, LANES))

    def look_up(index, groups):
        low, high = index & (LANES - 1), index >> 7
        acc = [jnp.zeros(index.shape, F32) for _ in groups]
        for r in range(rows_n * (COLS // LANES)):
            here = high == r
            for at, group in enumerate(groups):
                acc[at] = jnp.where(here, take_lanes(table[group, r], low), acc[at])
        return acc

    def one_hot_rows(low):
        iota = lax.broadcasted_iota(jnp.int32, (COLS, low.shape[1]), 0)
        return jnp.where(iota == low, 1.0, 0.0).astype(BF16)

    def site_prep():
        for h in range(rows_n):
            at = pl.ds(h * COLS, COLS)
            mass[h : h + 1] = mass_in[:, at]
            slot[h : h + 1] = slot_in[:, at]
            for c in range(3):
                u_now[c, h : h + 1] = now_in[c : c + 1, at]
                u_prev[c, h : h + 1] = prev_in[c : c + 1, at]
        free[...] = jnp.zeros(free.shape, F32)

        n_k = stiff.shape[0]
        n_r, n_c = kblock.shape
        ri = lax.broadcasted_iota(jnp.int32, (n_r, n_k), 0)
        rk = lax.broadcasted_iota(jnp.int32, (n_r, n_k), 1)
        pick_r = jnp.where(ri % n_k == rk, 1.0, 0.0)
        ck = lax.broadcasted_iota(jnp.int32, (n_k, n_c), 0)
        ci = lax.broadcasted_iota(jnp.int32, (n_k, n_c), 1)
        pick_c = jnp.where(ci % n_k == ck, 1.0, 0.0)
        exact = functools.partial(
            jnp.dot, precision=lax.Precision.HIGHEST, preferred_element_type=F32
        )
        tiled = exact(exact(pick_r, stiff[...]), pick_c)
        top, rest = split(tiled)
        rr = lax.broadcasted_iota(jnp.int32, (n_r, n_c), 0)
        cc = lax.broadcasted_iota(jnp.int32, (n_r, n_c), 1)
        part = (cc // n_k) % 3
        value = jnp.where(part == 2, rest, top)
        kblock[...] = jnp.where(rr // n_k == cc // (3 * n_k), value, 0.0).astype(BF16)

        def arrivals(p, carry):
            at = pl.ds(pl.multiple_of(p * LANES, LANES), LANES)
            node = recv_node[pl.ds(p, 1), :]
            oh_recv[:, at] = one_hot_rows(node & (COLS - 1))
            lhs[pl.ds(0, rows_n), at] = jnp.where((node >> 8) == high_iota, 1.0, 0.0).astype(BF16)
            return carry

        lax.fori_loop(0, n_dom, arrivals, 0)
        drm = lax.dot_general(
            lhs[pl.ds(0, rows_n), pl.ds(0, n_arr)], oh_recv[...], NT, preferred_element_type=F32
        )
        for h in range(rows_n):
            flag = flag_in[:, pl.ds(h * COLS, COLS)].astype(F32)
            code[h : h + 1] = drm[h : h + 1] * (1.0 + flag)
        build_table(code[...], 0)

        def element_codes(i, carry):
            at = pl.ds(pl.multiple_of(i * LANES, LANES), LANES)
            (got,) = look_up(elem[:, at], (0,))
            inn[:, at] = jnp.where(got == 1.0, 1.0, 0.0)
            out[:, at] = jnp.where(got == 2.0, 1.0, 0.0)
            return carry

        lax.fori_loop(0, n_el // LANES, element_codes, 0)

        for j in range(8):
            oh_elem[j] = one_hot_rows(elem[j : j + 1] & (COLS - 1))

        ri = lax.broadcasted_iota(jnp.int32, (16, COLS), 0)
        li = lax.broadcasted_iota(jnp.int32, (16, COLS), 1)
        found = jnp.zeros((16, COLS), F32)
        for h in range(rows_n):
            row = slot[h : h + 1]
            value = jnp.where(ri < 2, h, li)
            hit = ((row >> 8) == (ri & 1)) & (ri < 4)
            found = found + lax.dot_general(
                jnp.where(hit, value, 0).astype(F32).astype(BF16),
                one_hot_rows(row & (COLS - 1)),
                NT,
                preferred_element_type=F32,
            )
        slot_node[...] = jnp.full(slot_node.shape, -1, jnp.int32)
        for r in range(2 * SHARE // LANES):
            at = slice((r % 2) * LANES, (r % 2 + 1) * LANES)
            side = r // 2
            node = found[side : side + 1, at] * COLS + found[2 + side : 3 + side, at]
            slot_node[r : r + 1] = node.astype(jnp.int32)

    def place(k):
        def body(p, carry):
            at = pl.ds(pl.multiple_of(p * LANES, LANES), LANES)
            here = (recv_node[pl.ds(p, 1), :] >> 8) == high_iota
            got = samp_recv[k, p]
            for c in range(3):
                for s, part in enumerate(split(got[c : c + 1])):
                    lhs[pl.ds((2 * c + s) * rows_n, rows_n), at] = jnp.where(
                        here, part, 0.0
                    ).astype(BF16)
            return carry

        lax.fori_loop(0, n_dom, body, 0)
        placed = lax.dot_general(
            lhs[:, pl.ds(0, n_arr)], oh_recv[...], NT, preferred_element_type=F32
        )
        for c in range(3):
            at = 2 * c * rows_n
            free[c] = free[c] + DT * (placed[at : at + rows_n] + placed[at + rows_n : at + 2 * rows_n])

    def element_forces():
        for c in range(3):
            build_table(u_now[c], c)
            build_table(free[c], 3 + c)

        def body(i, carry):
            at = pl.ds(pl.multiple_of(i * LANES, LANES), LANES)
            got = look_up(elem[:, at], range(6))
            inner, outer = inn[:, at], out[:, at]
            blocks = []
            for group in (got[:3], [g * inner for g in got[3:]], [g * outer for g in got[3:]]):
                parts = [split(g) for g in group]
                tops = [t for t, _ in parts]
                blocks += tops + [r for _, r in parts] + tops
            blocks.append(jnp.zeros((8, LANES), F32))
            cols[:, at] = jnp.concatenate(blocks, axis=0).astype(BF16)
            return carry

        lax.fori_loop(0, n_el // LANES, body, 0)
        for part in range(n_el // 512):
            at = pl.ds(part * 512, 512)
            response = jnp.dot(kblock[...], cols[:, at], preferred_element_type=F32)
            inner, outer, mod = inn[:, at], out[:, at], modulus[:, at]
            for c in range(3):
                a = 8 * c
                value = mod * (
                    -response[a : a + 8]
                    + outer * response[24 + a : 32 + a]
                    - inner * response[48 + a : 56 + a]
                )
                fe[0, pl.ds(a, 8), at], fe[1, pl.ds(a, 8), at] = split(value)

        total = jnp.zeros((6 * rows_n, COLS), F32)
        wide_iota = lax.broadcasted_iota(jnp.int32, (rows_n, n_el), 0)
        for j in range(8):
            here = (elem[j : j + 1] >> 8) == wide_iota
            for c in range(3):
                for s in range(2):
                    lhs[pl.ds((2 * c + s) * rows_n, rows_n), pl.ds(0, n_el)] = jnp.where(
                        here, fe[s, 8 * c + j : 8 * c + j + 1], 0.0
                    ).astype(BF16)
            total = total + lax.dot_general(
                lhs[:, pl.ds(0, n_el)], oh_elem[j], NT, preferred_element_type=F32
            )
        for c in range(3):
            at = 2 * c * rows_n
            force[c] = total[at : at + rows_n] + total[at + rows_n : at + 2 * rows_n]

    def rim_copy(k, side):
        there = lax.rem(me_d + (n_dom - 1 if side == 0 else 1), n_dom)
        return pltpu.make_async_remote_copy(
            src_ref=rim_send.at[k, side],
            dst_ref=rim_recv.at[k, 1 - side],
            send_sem=r_send_sem.at[k, side],
            recv_sem=r_recv_sem.at[k, 1 - side],
            device_id=(me_s, there),
            device_id_type=MESH,
        )

    def rim_start(k):
        for c in range(3):
            build_table(force[c], c)
        got = look_up(slot_node[...], range(3))
        for side in range(2):
            for c in range(3):
                rim_send[k, side, 2 * c : 2 * c + 2, :] = got[c][2 * side : 2 * side + 2]
            rim_copy(k, side).start()

    def rim_finish(k):
        for side in range(2):
            rim_copy(k, side).wait_send()
            rim_copy(k, 1 - side).wait_recv()
        for half in range(COLS // LANES):
            at = slice(half * LANES, (half + 1) * LANES)
            index = slot[:, at]
            low, high = index & (LANES - 1), index >> 7
            for c in range(3):
                value = force[c, :, at]
                extra = jnp.zeros(value.shape, F32)
                for r in range(2 * SHARE // LANES):
                    row = rim_recv[k, r // 2, 2 * c + r % 2 : 2 * c + r % 2 + 1, :]
                    got = take_lanes(jnp.broadcast_to(row, index.shape), low)
                    extra = jnp.where(high == r, got, extra)
                u = u_now[c, :, at]
                following = (2.0 * u - u_prev[c, :, at]) + DT_SITE2 * (value + extra) / mass[:, at]
                u_prev[c, :, at] = u
                u_now[c, :, at] = following

    def first_pack(x, carry):
        y_pack(0, STRESS_Y, x, {f: st[f, x + 2] for f, _ in STRESS_Y})
        return carry

    lax.fori_loop(0, cx, first_pack, 0)
    expected = (
        n_dom - 1 + jnp.where(me_s > 0, 1, 0) + jnp.where(me_s < n_site - 1, 1, 0)
    ).astype(jnp.int32)
    pl.semaphore_wait(barrier, expected)
    halo_start(0, STRESS_X, STRESS_Y)
    site_prep()
    for k in range(STEPS):
        halo_wait(0, STRESS_X, STRESS_Y)
        velocity_half()
        halo_start(1, VEL_X, VEL_Y)
        sample(k)
        sample_start(k)
        if k:
            rim_finish(k - 1)
        halo_wait(1, VEL_X, VEL_Y)
        stress_half()
        if k < STEPS - 1:
            halo_start(0, STRESS_X, STRESS_Y)
        else:
            store = pltpu.make_async_copy(st.at[:, pl.ds(2, cx)], basin_out, out_sem)
            store.start()
        sample_wait(k)
        place(k)
        element_forces()
        rim_start(k)
    rim_finish(STEPS - 1)
    for h in range(rows_n):
        for c in range(3):
            disp_out[c : c + 1, pl.ds(h * COLS, COLS)] = u_now[c, h : h + 1]
    store.wait()


def solution(mesh):
    n_site, n_dom = mesh.shape["site"], mesh.shape["dom"]

    def on_device(
        fields, material, send_cell, recv_node, elements, modulus, node_mass, outer_flag, shared_slot, stiffness,
        disp_now, disp_prev,
    ):
        _, cx, cy, nz = fields.shape
        n_nodes = disp_now.shape[3]
        n_el = elements.shape[3]
        rows_n = n_nodes // COLS
        n_arr = n_dom * LANES
        vmem = pl.BlockSpec(memory_space=pltpu.VMEM)
        hbm = pl.BlockSpec(memory_space=pl.ANY)
        sem = pltpu.SemaphoreType.DMA
        node3 = pltpu.VMEM((3, rows_n, COLS), F32)
        basin, disp = pl.pallas_call(
            functools.partial(kernel, n_site, n_dom),
            out_shape=(
                jax.ShapeDtypeStruct(fields.shape, F32),
                jax.ShapeDtypeStruct((3, n_nodes), F32),
            ),
            in_specs=[hbm] + [vmem] * 11,
            out_specs=(hbm, vmem),
            scratch_shapes=[
                pltpu.VMEM((9, cx + 4, cy, nz), F32),
                pltpu.VMEM((2, 6, cx, nz), F32),
                pltpu.VMEM((2, 6, cx, nz), F32),
                pltpu.VMEM((2, 6, cx, nz), F32),
                pltpu.VMEM((2, 6, cx, nz), F32),
                pltpu.VMEM((STEPS, n_dom, 3, LANES), F32),
                pltpu.VMEM((STEPS, n_dom, 3, LANES), F32),
                pltpu.VMEM((STEPS, 2, 8, LANES), F32),
                pltpu.VMEM((STEPS, 2, 8, LANES), F32),
                pltpu.VMEM((COLS, n_arr), BF16),
                pltpu.VMEM((8, COLS, n_el), BF16),
                pltpu.VMEM((6 * rows_n, max(n_el, n_arr)), BF16),
                pltpu.VMEM((6, n_nodes // LANES, 8, LANES), F32),
                pltpu.VMEM((8, n_el), F32),
                pltpu.VMEM((8, n_el), F32),
                pltpu.VMEM((224, n_el), BF16),
                pltpu.VMEM((72, 224), BF16),
                pltpu.VMEM((2, 24, n_el), F32),
                node3,
                node3,
                node3,
                pltpu.VMEM((rows_n, COLS), F32),
                pltpu.VMEM((rows_n, COLS), F32),
                pltpu.VMEM((rows_n, COLS), jnp.int32),
                pltpu.VMEM((8, LANES), jnp.int32),
                node3,
                sem,
                sem,
                sem((2, 2, 3)),
                sem((2, 2, 3)),
                sem((2, 2)),
                sem((2, 2)),
                sem((STEPS, n_dom)),
                sem((STEPS, n_dom)),
                sem((STEPS, 2)),
                sem((STEPS, 2)),
            ],
            compiler_params=pltpu.CompilerParams(
                collective_id=0, has_side_effects=True, vmem_limit_bytes=48 * 1024 * 1024
            ),
        )(
            fields, material, send_cell[0, 0], recv_node[0, 0], elements[0, 0], modulus[0], node_mass[0], outer_flag[0],
            shared_slot[0], stiffness, disp_now[0, 0], disp_prev[0, 0],
        )
        return basin, disp[None, None]

    spread3 = P("site", "dom", None)
    spread4 = P("site", "dom", None, None)
    slab = P(None, "dom", "site", None)
    return jax.shard_map(
        on_device,
        mesh=mesh,
        in_specs=(
            slab, slab, spread4, spread4, spread4, spread3, spread3, spread3, spread3, P(), spread4, spread4,
        ),
        out_specs=(slab, spread4),
        check_vma=False,
    )
```

time: 1440 us -> 86.9 us (0.06)
  the two profiles are of different devices: /device:TPU:97 before, /device:TPU:7 now
where the time goes in v1:
time: 86.9 us; the launch traced here: 86.3 us
  Pallas kernels  75 us (86%)
  local copies, waits for them, and re-layouts  10.6 us (12%)
    pallas_call x1, Pallas kernels, on_device(): pl.pallas_call(functools.partial(kernel, n_site, n_dom), out_shape=(jax.S...  75 us
    unnamed x23, local copies, waits for them, and re-layouts  10.6 us

profile of v1, /device:TPU:7, one launch (start us, length us, event | category | flops | bytes accessed | tf_op | source)
XLA Modules:
  0.0 86.3 jit_solution(12878858279849121213)
XLA Ops:
  0.6 0.9 %copy_bitcast_fusion = (f32[3,4096]{1,0:T(4,128)S(1)}, f32[3,4096]{1,0:T(4,128)S(1)}) fusion(f32[1,1,3,4096]{3,1,2,0:T(1,128)} %param.23, f32[1,1,3,4096]{3,1,2,0:T(1,128)} %param.22), kind=kLoop, calls=%fused_computation | loop fusion | bytes 196608
  1.5 0.0 copy-start
  1.5 1.3 %copy-done = f32[9,8,16,256]{3,2,1,0:T(8,128)S(1)} copy-done((f32[9,8,16,256]{3,2,1,0:T(8,128)S(1)}, f32[9,8,16,256]{3,2,1,0:T(8,128)}, u32[]{:S(2)}) %copy-start) | copy-done | bytes 1179672
  2.8 0.0 copy-start.1
  2.8 1.0 %copy-done.1 = f32[3,8,16,256]{3,2,1,0:T(8,128)S(1)} copy-done((f32[3,8,16,256]{3,2,1,0:T(8,128)S(1)}, f32[3,8,16,256]{3,2,1,0:T(8,128)}, u32[]{:S(2)}) %copy-start.1) | copy-done | bytes 393240
  3.8 0.0 copy-start.2
  3.8 0.8 copy-done.2
  4.6 0.0 copy-start.3
  4.6 0.7 copy-done.3
  5.4 0.0 copy-start.4
  5.4 0.7 copy-done.4
  6.1 0.0 copy-start.5
  6.1 0.7 copy-done.5
  6.8 0.0 copy-start.6
  6.8 0.7 copy-done.6
  7.5 0.0 copy-start.7
  7.5 0.7 copy-done.7
  8.2 0.0 copy-start.8
  8.2 0.7 copy-done.8
  8.9 0.0 copy-start.9
  8.9 0.7 copy-done.9
  9.6 75.0 %shard_map.131 = (f32[9,8,16,256]{3,2,1,0:T(8,128)S(1)}, f32[3,4096]{1,0:T(4,128)S(1)}) custom-call(f32[9,8,16,256]{3,2,1,0:T(8,128)S(1)} %copy-done, f32[3,8,16,256]{3,2,1,0:T(8,128)S(1)} %copy-done.1, s32[16,128]{1,0:T(8,128)S(1)} %bitcast.17, s32[16,128]{1,0:T(8,128)S(1)} %bitcast.18, s32[8,2048]{1,0:T(8,128)S(1)} %bitcast.12, f32[1,2048]{1,0:T(1,128)S(1)} %bitcast.19, ...), custom_call_target="tpu_custom_call" | custom-call | tf_op jit(solution)/shard_map/pallas_call | solution.py:631
  84.6 0.7 copy.14
  85.3 1.0 %copy.20 = f32[9,8,16,256]{3,2,1,0:T(8,128)} copy(f32[9,8,16,256]{3,2,1,0:T(8,128)S(1)} %get-tuple-element.12) | data formatting | bytes 2359296
Async XLA Ops:
  1.5 1.3 %copy-start = (f32[9,8,16,256]{3,2,1,0:T(8,128)S(1)}, f32[9,8,16,256]{3,2,1,0:T(8,128)}, u32[]{:S(2)}) copy-start(f32[9,8,16,256]{3,2,1,0:T(8,128)} %fields.1) | copy-start | bytes 3538948
  2.8 1.0 %copy-start.1 = (f32[3,8,16,256]{3,2,1,0:T(8,128)S(1)}, f32[3,8,16,256]{3,2,1,0:T(8,128)}, u32[]{:S(2)}) copy-start(f32[3,8,16,256]{3,2,1,0:T(8,128)} %mat.1) | copy-start | bytes 1179652
  3.8 0.8 copy-start.2
  4.6 0.7 copy-start.3
  5.4 0.7 copy-start.4
  6.1 0.7 copy-start.5
  6.8 0.7 copy-start.6
  7.5 0.7 copy-start.7
  8.2 0.7 copy-start.8
  8.9 0.7 copy-start.9

commit v2 on v1

v2 whole, which is shorter than its diff:
```python
import functools

import jax
import jax.numpy as jnp
from jax import lax
from jax.experimental import pallas as pl
from jax.experimental.pallas import tpu as pltpu
from jax.sharding import PartitionSpec as P

STEPS = 3
SHARE = 256
C_NEAR = 9.0 / 8.0
C_FAR = 1.0 / 24.0
DT = 0.25
DT_SITE2 = 0.15
MESH = pl.DeviceIdType.MESH
LANES = 128
COLS = 256
F32 = jnp.float32
BF16 = jnp.bfloat16

STRESS_X = ((3, "F"), (6, "B"), (7, "B"))
STRESS_Y = ((6, "B"), (4, "F"), (8, "B"))
VEL_X = ((0, "B"), (1, "F"), (2, "F"))
VEL_Y = ((0, "F"), (1, "B"), (2, "F"))
LOW = {"B": 2, "F": 1}
HIGH = {"B": 1, "F": 2}


def take_lanes(table, lanes):
    return lax.gather(
        table,
        lanes[..., None],
        lax.GatherDimensionNumbers(
            offset_dims=(),
            collapsed_slice_dims=(1,),
            start_index_map=(1,),
            operand_batching_dims=(0,),
            start_indices_batching_dims=(0,),
        ),
        (1, 1),
        mode=lax.GatherScatterMode.PROMISE_IN_BOUNDS,
    )


def stencil(kind, m2, m1, f, p1, p2):
    if kind == "B":
        return C_NEAR * (f - m1) - C_FAR * (p1 - m2)
    return C_NEAR * (p1 - f) - C_FAR * (p2 - m1)


def diff_rolled(kind, f, axis, index, low, high):
    n = f.shape[axis]
    below = lambda v, edge: jnp.where(index == 0, edge, pltpu.roll(v, 1, axis))
    above = lambda v, edge: jnp.where(index == n - 1, edge, pltpu.roll(v, n - 1, axis))
    m1 = below(f, low[-1])
    p1 = above(f, high[0])
    if kind == "B":
        return stencil(kind, below(m1, low[0]), m1, f, p1, None)
    return stencil(kind, None, m1, f, p1, above(p1, high[1]))


def split(v):
    top = v.astype(BF16).astype(F32)
    return top, v - top


def kernel(
    n_site,
    n_dom,
    fields,
    mat_hbm,
    send_cell_hbm,
    recv_node_hbm,
    elem_hbm,
    modulus_hbm,
    mass_in_hbm,
    flag_in_hbm,
    slot_in_hbm,
    stiff_hbm,
    now_in_hbm,
    prev_in_hbm,
    basin_out,
    disp_out,
    mat,
    send_cell,
    recv_node,
    elem,
    modulus,
    mass_in,
    flag_in,
    slot_in,
    stiff,
    now_in,
    prev_in,
    disp_v,
    st,
    y_low,
    y_high,
    y_to_low,
    y_to_high,
    samp_send,
    samp_recv,
    rim_send,
    rim_recv,
    oh_recv,
    oh_recv_t,
    oh_elem,
    oh_elem_t,
    oh_slot,
    oh_slot_t,
    oh_cell,
    high_rows,
    lhs,
    inn,
    out,
    cols,
    kblock,
    node,
    prev,
    slot_node,
    force,
    in_sem,
    out_sem,
    in_sems,
    x_send_sem,
    x_recv_sem,
    y_send_sem,
    y_recv_sem,
    s_send_sem,
    s_recv_sem,
    r_send_sem,
    r_recv_sem,
):
    cx, cy, nz = mat.shape[1:]
    n_nodes = node.shape[1]
    runs = n_nodes // COLS
    n_el = elem.shape[1]
    n_arr = n_dom * LANES
    me_s = lax.axis_index("site")
    me_d = lax.axis_index("dom")

    load = pltpu.make_async_copy(fields, st.at[:, pl.ds(2, cx)], in_sem)
    load.start()
    inputs = [
        pltpu.make_async_copy(src, dst, in_sems.at[i])
        for i, (src, dst) in enumerate(
            (
                (mat_hbm, mat),
                (send_cell_hbm, send_cell),
                (recv_node_hbm, recv_node),
                (elem_hbm, elem),
                (modulus_hbm, modulus),
                (mass_in_hbm, mass_in),
                (flag_in_hbm, flag_in),
                (slot_in_hbm, slot_in),
                (stiff_hbm, stiff),
                (now_in_hbm, now_in),
                (prev_in_hbm, prev_in),
            )
        )
    ]
    for copy in inputs:
        copy.start()
    st[:, pl.ds(0, 2)] = jnp.zeros((9, 2, cy, nz), F32)
    st[:, pl.ds(2 + cx, 2)] = jnp.zeros((9, 2, cy, nz), F32)
    y_low[...] = jnp.zeros(y_low.shape, F32)
    y_high[...] = jnp.zeros(y_high.shape, F32)

    barrier = pltpu.get_barrier_semaphore()

    def greet(d, carry):
        pl.semaphore_signal(
            barrier, inc=1, device_id=(me_s, lax.rem(me_d + d, n_dom)), device_id_type=MESH
        )
        return carry

    lax.fori_loop(1, n_dom, greet, 0)
    for step in (-1, 1):
        there = me_s + step

        @pl.when((there >= 0) & (there < n_site))
        def _():
            pl.semaphore_signal(barrier, inc=1, device_id=(there, me_d), device_id_type=MESH)

    load.wait()
    for copy in inputs:
        copy.wait()

    row_iota = lax.broadcasted_iota(jnp.int32, (cy, nz), 0)
    lane_iota = lax.broadcasted_iota(jnp.int32, (cy, nz), 1)

    def x_copies(which, fields_x, upward):
        made = []
        for at, (f, kind) in enumerate(fields_x):
            if upward:
                width = LOW[kind]
                src = st.at[f, pl.ds(2 + cx - width, width)]
                dst = st.at[f, pl.ds(2 - width, width)]
                there = me_d + 1
            else:
                width = HIGH[kind]
                src = st.at[f, pl.ds(2, width)]
                dst = st.at[f, pl.ds(2 + cx, width)]
                there = me_d - 1
            sem = (which, 1 if upward else 0, at)
            made.append(
                pltpu.make_async_remote_copy(
                    src_ref=src,
                    dst_ref=dst,
                    send_sem=x_send_sem.at[sem],
                    recv_sem=x_recv_sem.at[sem],
                    device_id=(me_s, there),
                    device_id_type=MESH,
                )
            )
        return made

    def y_copy(which, fields_y, upward):
        count = sum((LOW if upward else HIGH)[kind] for _, kind in fields_y)
        src, dst = (y_to_high, y_low) if upward else (y_to_low, y_high)
        sem = (which, 1 if upward else 0)
        return pltpu.make_async_remote_copy(
            src_ref=src.at[which, pl.ds(0, count)],
            dst_ref=dst.at[which, pl.ds(0, count)],
            send_sem=y_send_sem.at[sem],
            recv_sem=y_recv_sem.at[sem],
            device_id=(me_s + (1 if upward else -1), me_d),
            device_id_type=MESH,
        )

    has = {
        "x": (me_d > 0, me_d < n_dom - 1),
        "y": (me_s > 0, me_s < n_site - 1),
    }

    def halo_start(which, fields_x, fields_y):
        for upward in (False, True):

            @pl.when(has["x"][upward])
            def _():
                for copy in x_copies(which, fields_x, upward):
                    copy.start()

            @pl.when(has["y"][upward])
            def _():
                y_copy(which, fields_y, upward).start()

    def halo_wait(which, fields_x, fields_y):
        for upward in (False, True):

            @pl.when(has["x"][upward])
            def _():
                for copy in x_copies(which, fields_x, upward):
                    copy.wait_send()

            @pl.when(has["x"][not upward])
            def _():
                for copy in x_copies(which, fields_x, upward):
                    copy.wait_recv()

            @pl.when(has["y"][upward])
            def _():
                y_copy(which, fields_y, upward).wait_send()

            @pl.when(has["y"][not upward])
            def _():
                y_copy(which, fields_y, upward).wait_recv()

    def y_pack(which, fields_y, x, planes):
        at = 0
        for f, kind in fields_y:
            for k in range(LOW[kind]):
                y = cy - LOW[kind] + k
                y_to_high[which, at, pl.ds(x, 1), :] = planes[f][y : y + 1]
                at += 1
        at = 0
        for f, kind in fields_y:
            for k in range(HIGH[kind]):
                y_to_low[which, at, pl.ds(x, 1), :] = planes[f][k : k + 1]
                at += 1

    def y_edges(which, fields_y, x):
        edges = {}
        low_at = high_at = 0
        for f, kind in fields_y:
            low = [y_low[which, low_at + k, pl.ds(x, 1), :] for k in range(LOW[kind])]
            high = [y_high[which, high_at + k, pl.ds(x, 1), :] for k in range(HIGH[kind])]
            low_at += LOW[kind]
            high_at += HIGH[kind]
            edges[f] = (low, high)
        return edges

    def diff_x(kind, f, x):
        at = lambda o: st[f, x + 2 + o]
        if kind == "B":
            return stencil(kind, at(-2), at(-1), at(0), at(1), None)
        return stencil(kind, None, at(-1), at(0), at(1), at(2))

    def diff_y(kind, f, x, edges):
        low, high = edges[f]
        return diff_rolled(kind, st[f, x + 2], 0, row_iota, low, high)

    def diff_z(kind, f, x):
        return diff_rolled(kind, st[f, x + 2], 1, lane_iota, (0.0, 0.0), (0.0, 0.0))

    def velocity_half():
        def body(x, carry):
            edges = y_edges(0, STRESS_Y, x)
            b = DT * mat[0, x]
            planes = {
                0: st[0, x + 2]
                + b * (diff_x("F", 3, x) + diff_y("B", 6, x, edges) + diff_z("B", 7, x)),
                1: st[1, x + 2]
                + b * (diff_x("B", 6, x) + diff_y("F", 4, x, edges) + diff_z("B", 8, x)),
                2: st[2, x + 2]
                + b * (diff_x("B", 7, x) + diff_y("B", 8, x, edges) + diff_z("F", 5, x)),
            }
            for f, plane in planes.items():
                st[f, x + 2] = plane
            y_pack(1, VEL_Y, x, planes)
            return carry

        lax.fori_loop(0, cx, body, 0)

    def stress_half():
        def body(x, carry):
            edges = y_edges(1, VEL_Y, x)
            lam, mu = mat[1, x], mat[2, x]
            exx = diff_x("B", 0, x)
            eyy = diff_y("B", 1, x, edges)
            ezz = diff_z("B", 2, x)
            wide = lam + 2.0 * mu
            shear = DT * mu
            planes = {
                3: st[3, x + 2] + DT * (wide * exx + lam * (eyy + ezz)),
                4: st[4, x + 2] + DT * (wide * eyy + lam * (exx + ezz)),
                5: st[5, x + 2] + DT * (wide * ezz + lam * (exx + eyy)),
                6: st[6, x + 2] + shear * (diff_y("F", 0, x, edges) + diff_x("F", 1, x)),
                7: st[7, x + 2] + shear * (diff_z("F", 0, x) + diff_x("F", 2, x)),
                8: st[8, x + 2] + shear * (diff_z("F", 1, x) + diff_y("F", 2, x, edges)),
            }
            for f, plane in planes.items():
                st[f, x + 2] = plane
            y_pack(0, STRESS_Y, x, planes)
            return carry

        lax.fori_loop(0, cx, body, 0)

    def sample(k):
        n = n_arr // 2
        for i in range(2):
            cell = [send_cell[q : q + 1] for q in range(i * n_dom // 2, (i + 1) * n_dom // 2)]
            high = jnp.concatenate([jnp.broadcast_to(v >> 8, (8, LANES)) for v in cell], axis=1)
            row = lax.broadcasted_iota(jnp.int32, high.shape, 0)
            for c in range(3):
                parts = split(st[c, pl.ds(2, cx)].reshape(cx * cy, nz))
                table = jnp.concatenate(parts, axis=0).astype(BF16)
                found = jnp.dot(table, oh_cell[:, pl.ds(i * n, n)], preferred_element_type=F32)
                total = jnp.zeros(high.shape, F32)
                for t in range(cx * cy // 8):
                    both = found[8 * t : 8 * t + 8] + found[cx * cy + 8 * t : cx * cy + 8 * t + 8]
                    total = jnp.where(high == row + 8 * t, both, total)
                total = jnp.sum(total, axis=0, keepdims=True)
                for q in range(n_dom // 2):
                    samp_send[k, i * n_dom // 2 + q, c : c + 1, :] = total[
                        :, q * LANES : (q + 1) * LANES
                    ]

    def sample_copy(k, d):
        there = lax.rem(me_d + d, n_dom)
        return pltpu.make_async_remote_copy(
            src_ref=samp_send.at[k, there],
            dst_ref=samp_recv.at[k, me_d],
            send_sem=s_send_sem.at[k, d],
            recv_sem=s_recv_sem.at[k, d],
            device_id=(me_s, there),
            device_id_type=MESH,
        )

    def sample_start(k):
        def body(d, carry):
            sample_copy(k, d).start()
            return carry

        lax.fori_loop(1, n_dom, body, 0)
        samp_recv[k, me_d] = samp_send[k, me_d]

    def sample_wait(k):
        def body(d, carry):
            here = lax.rem(me_d + n_dom - d, n_dom)
            copy = pltpu.make_async_remote_copy(
                src_ref=samp_send.at[k, here],
                dst_ref=samp_recv.at[k, here],
                send_sem=s_send_sem.at[k, d],
                recv_sem=s_recv_sem.at[k, d],
                device_id=(me_s, here),
                device_id_type=MESH,
            )
            copy.wait_recv()
            sample_copy(k, d).wait_send()
            return carry

        lax.fori_loop(1, n_dom, body, 0)

    def run(h):
        return pl.ds(h * COLS, COLS)

    def by_run(value):
        return jnp.concatenate([value[:, h * COLS : (h + 1) * COLS] for h in range(runs)], axis=0)

    def by_node(value):
        return jnp.concatenate([value[8 * h : 8 * h + 8] for h in range(runs)], axis=1)

    def packed(row):
        return jnp.broadcast_to(row.astype(F32), (16, row.shape[1])).astype(BF16)

    def one_hot(low, ref):
        low16 = packed(low)
        iota = lax.broadcasted_iota(jnp.int32, low16.shape, 0).astype(F32).astype(BF16)
        one, zero = jnp.ones(low16.shape, BF16), jnp.zeros(low16.shape, BF16)
        for t in range(COLS // 16):
            ref[pl.ds(16 * t, 16), :] = jnp.where(iota + BF16(16 * t) == low16, one, zero)

    def one_hot_both(low, ref, turned):
        one_hot(low, ref)
        turned[...] = ref[...].T

    def spread(high, values, ref):
        high16 = packed(high)
        twice = jnp.concatenate([values, values], axis=0).astype(BF16)
        second = (lax.broadcasted_iota(jnp.int32, high16.shape, 0) >> 3).astype(F32).astype(BF16)
        zero = jnp.zeros(high16.shape, BF16)
        for t in range(runs // 2):
            ref[pl.ds(16 * t, 16), :] = jnp.where(second + BF16(2 * t) == high16, twice, zero)

    def sub(shape):
        return lax.broadcasted_iota(jnp.int32, shape, 0) & 7

    def prep_nodes():
        node[...] = jnp.zeros(node.shape, F32)
        prev[...] = jnp.zeros(prev.shape, F32)
        for c in range(3):
            node[c : c + 1, :] = now_in[c]
            prev[c : c + 1, :] = prev_in[c]

    def prep_k():
        n_k = stiff.shape[0]
        n_r, n_c = kblock.shape

        def dof(i, comp):
            return comp * 8 + ((i & 63) >> 3)

        def comp3(i):
            r = i & 7
            return jnp.where(r < 3, r, r - 3)

        ri = lax.broadcasted_iota(jnp.int32, (n_r, n_k), 0)
        rk = lax.broadcasted_iota(jnp.int32, (n_r, n_k), 1)
        pick_r = jnp.where((dof(ri, comp3(ri)) == rk) & ((ri & 7) < 6), 1.0, 0.0)
        ck = lax.broadcasted_iota(jnp.int32, (n_k, n_c), 0)
        ci = lax.broadcasted_iota(jnp.int32, (n_k, n_c), 1)
        pick_c = jnp.where((dof(ci, comp3(ci)) == ck) & ((ci & 7) < 6), 1.0, 0.0)
        exact = functools.partial(
            jnp.dot, precision=lax.Precision.HIGHEST, preferred_element_type=F32
        )
        top, rest = split(exact(exact(pick_r, stiff[...]), pick_c))
        group = lax.broadcasted_iota(jnp.int32, (n_r, n_c), 0) >> 6
        ci = lax.broadcasted_iota(jnp.int32, (n_r, n_c), 1)
        block, free_col = ci >> 6, (ci & 7) >= 3
        outer_block = (block == 2) | (block == 3) | (block == 5)
        inner_block = (block == 0) | (block == 1) | (block == 4)
        meant = (
            ((group == 0) & ((ci & 7) < 3) & inner_block)
            | ((group == 1) & free_col & inner_block)
            | ((group == 2) & free_col & outer_block)
        )
        value = jnp.where(block >= 4, rest, top)
        value = jnp.where(group == 1, value, -value)
        kblock[...] = jnp.where(meant, value, 0.0).astype(BF16)

    def prep_arr():
        for p in range(n_dom):
            at = pl.ds(p * LANES, LANES)
            one_hot_both(recv_node[p : p + 1] & (COLS - 1), oh_recv.at[:, at], oh_recv_t.at[at])

    def prep_hot():
        for j in range(8):
            one_hot_both(elem[j : j + 1] & (COLS - 1), oh_elem.at[j], oh_elem_t.at[j])
            high_rows[j] = jnp.broadcast_to(elem[j : j + 1] >> 8, (8, n_el))

    def prep_cell():
        for q in range(n_dom):
            one_hot(send_cell[q : q + 1] & (nz - 1), oh_cell.at[:, pl.ds(q * LANES, LANES)])

    def prep_slot():
        row = slot_in[...]
        one_hot_both(row & (COLS - 1), oh_slot, oh_slot_t)
        ri = lax.broadcasted_iota(jnp.int32, (16, n_nodes), 0)
        li = lax.broadcasted_iota(jnp.int32, (16, n_nodes), 1)
        value = jnp.where(ri < 2, li >> 8, li & (COLS - 1))
        hit = ((row >> 8) == (ri & 1)) & (ri < 4)
        found = jnp.dot(
            jnp.where(hit, value, 0).astype(F32).astype(BF16),
            oh_slot_t[...],
            preferred_element_type=F32,
        )
        for r in range(2 * SHARE // LANES):
            at = slice((r % 2) * LANES, (r % 2 + 1) * LANES)
            side = r // 2
            where = found[side : side + 1, at] * COLS + found[2 + side : 3 + side, at]
            slot_node[r] = jnp.broadcast_to(where.astype(jnp.int32), (8, LANES))

    def place(k):
        for p in range(n_dom):
            got = samp_recv[k, p]
            top, rest = split(got)
            values = jnp.concatenate([rest, top, jnp.ones((2, LANES), F32)], axis=0)
            spread(recv_node[p : p + 1] >> 8, values, lhs.at[0, :, pl.ds(p * LANES, LANES)])
        placed = by_node(
            jnp.dot(lhs[0, :, pl.ds(0, n_arr)], oh_recv_t[...], preferred_element_type=F32)
        )
        old, row = node[...], sub(node.shape)
        both = placed + pltpu.roll(placed, 3, 0)
        new = jnp.where((row >= 3) & (row < 6), old + DT * both, old)
        if k == 0:
            flag = flag_in[...].astype(F32)
            share = jnp.where(row == 7, flag, 1.0 - flag)
            new = jnp.where(row >= 6, placed * share, new)
        node[...] = new

    def element_cols(k):
        top, rest = split(by_run(node[...]))
        table = jnp.concatenate([top, rest], axis=0).astype(BF16)
        first = sub((8, COLS)) < 3
        for i in range(n_el // COLS):
            at = pl.ds(i * COLS, COLS)
            for pair in range(4):
                with_inner, with_outer = [], []
                for j in (2 * pair, 2 * pair + 1):
                    found = jnp.dot(table, oh_elem[j, :, at], preferred_element_type=F32)
                    high = high_rows[j, :, at]
                    got = jnp.zeros((8, COLS), F32)
                    for h in range(runs):
                        both = found[8 * h : 8 * h + 8] + found[8 * (runs + h) : 8 * (runs + h) + 8]
                        got = jnp.where(high == h, both, got)
                    if k == 0:
                        inn[j, :, at] = jnp.broadcast_to(got[6:7], got.shape)
                        out[j, :, at] = jnp.broadcast_to(got[7:8], got.shape)
                    with_inner.append(jnp.where(first, got, got * inn[j, :, at]))
                    with_outer.append(got * out[j, :, at])
                blocks = split(jnp.concatenate(with_inner, axis=0))
                blocks += split(jnp.concatenate(with_outer, axis=0))
                blocks += (blocks[0], blocks[2])
                for which, block in enumerate(blocks):
                    cols[pl.ds(64 * which + 16 * pair, 16), at] = block.astype(BF16)

    def element_response():
        wide = n_el // 2
        first = sub((8, wide)) < 3
        for i in range(2):
            at = pl.ds(i * wide, wide)
            response = jnp.dot(kblock[...], cols[:, at], preferred_element_type=F32)
            mod = jnp.broadcast_to(modulus[:, at], (8, wide))
            for j in range(8):
                value = mod * (
                    response[8 * j : 8 * j + 8]
                    + out[j, :, at] * response[64 + 8 * j : 72 + 8 * j]
                    + inn[j, :, at] * response[128 + 8 * j : 136 + 8 * j]
                )
                top, rest = split(value)
                spread(elem[j : j + 1, at] >> 8, jnp.where(first, top, rest), lhs.at[j, :, at])

    def element_add():
        total = jnp.zeros((8 * runs, COLS), F32)
        for j in range(8):
            total = total + jnp.dot(
                lhs[j, :, pl.ds(0, n_el)], oh_elem_t[j], preferred_element_type=F32
            )
        both = by_node(total)
        force[...] = both + pltpu.roll(both, 5, 0)

    def rim_copy(k, side):
        there = lax.rem(me_d + (n_dom - 1 if side == 0 else 1), n_dom)
        return pltpu.make_async_remote_copy(
            src_ref=rim_send.at[k, side],
            dst_ref=rim_recv.at[k, 1 - side],
            send_sem=r_send_sem.at[k, side],
            recv_sem=r_recv_sem.at[k, 1 - side],
            device_id=(me_s, there),
            device_id_type=MESH,
        )

    def rim_start(k):
        for side in range(2):
            for half in range(SHARE // LANES):
                index = slot_node[2 * side + half]
                low, high = index & (LANES - 1), index >> 7
                got = jnp.zeros((8, LANES), F32)
                for r in range(n_nodes // LANES):
                    piece = take_lanes(force[:, pl.ds(r * LANES, LANES)], low)
                    got = jnp.where(high == r, piece, got)
                rim_send[k, side, :, pl.ds(half * LANES, LANES)] = got[:3]
            rim_copy(k, side).start()

    def rim_finish(k):
        for side in range(2):
            rim_copy(k, side).wait_send()
            rim_copy(k, 1 - side).wait_recv()
        tables = []
        for r in range(2 * SHARE // LANES):
            got = rim_recv[k, r // 2, :, pl.ds((r % 2) * LANES, LANES)]
            tables.append(jnp.concatenate([got, jnp.zeros((5, LANES), F32)], axis=0))
        for i in range(n_nodes // LANES):
            at = pl.ds(i * LANES, LANES)
            index = jnp.broadcast_to(slot_in[:, at], (8, LANES))
            low, high = index & (LANES - 1), index >> 7
            extra = jnp.zeros((8, LANES), F32)
            for r, piece in enumerate(tables):
                extra = jnp.where(high == r, take_lanes(piece, low), extra)
            u = node[:, at]
            following = (2.0 * u - prev[:, at]) + DT_SITE2 * (force[:, at] + extra) / mass_in[:, at]
            prev[:, at] = u
            node[:, at] = jnp.where(sub(u.shape) < 3, following, u)

    def first_pack(x, carry):
        y_pack(0, STRESS_Y, x, {f: st[f, x + 2] for f, _ in STRESS_Y})
        return carry

    lax.fori_loop(0, cx, first_pack, 0)
    expected = (
        n_dom - 1 + jnp.where(me_s > 0, 1, 0) + jnp.where(me_s < n_site - 1, 1, 0)
    ).astype(jnp.int32)
    pl.semaphore_wait(barrier, expected)
    halo_start(0, STRESS_X, STRESS_Y)
    prep_nodes()
    prep_k()
    prep_arr()
    prep_hot()
    prep_slot()
    prep_cell()
    for k in range(STEPS):
        halo_wait(0, STRESS_X, STRESS_Y)
        velocity_half()
        halo_start(1, VEL_X, VEL_Y)
        sample(k)
        sample_start(k)
        if k:
            rim_finish(k - 1)
        halo_wait(1, VEL_X, VEL_Y)
        stress_half()
        if k < STEPS - 1:
            halo_start(0, STRESS_X, STRESS_Y)
        else:
            store = pltpu.make_async_copy(st.at[:, pl.ds(2, cx)], basin_out, out_sem)
            store.start()
        sample_wait(k)
        place(k)
        element_cols(k)
        element_response()
        element_add()
        rim_start(k)
    rim_finish(STEPS - 1)
    for c in range(3):
        disp_v[c] = node[c : c + 1, :]
    disp_store = pltpu.make_async_copy(disp_v, disp_out, in_sem)
    disp_store.start()
    disp_store.wait()
    store.wait()


def solution(mesh):
    n_site, n_dom = mesh.shape["site"], mesh.shape["dom"]

    def on_device(
        fields, material, send_cell, recv_node, elements, modulus, node_mass, outer_flag, shared_slot, stiffness,
        disp_now, disp_prev,
    ):
        _, cx, cy, nz = fields.shape
        n_nodes = disp_now.shape[3]
        n_el = elements.shape[3]
        runs = n_nodes // COLS
        n_arr = n_dom * LANES
        hbm = pl.BlockSpec(memory_space=pltpu.HBM)
        sem = pltpu.SemaphoreType.DMA
        operands = (
            fields, material, send_cell[0, 0], recv_node[0, 0], elements[0, 0], modulus[0], node_mass[0], outer_flag[0],
            shared_slot[0], stiffness, disp_now.reshape(3, 1, n_nodes), disp_prev.reshape(3, 1, n_nodes),
        )
        basin, disp = pl.pallas_call(
            functools.partial(kernel, n_site, n_dom),
            out_shape=(
                jax.ShapeDtypeStruct(fields.shape, F32),
                jax.ShapeDtypeStruct((3, 1, n_nodes), F32),
            ),
            in_specs=[hbm] * 12,
            out_specs=(hbm, hbm),
            scratch_shapes=[
                *(pltpu.VMEM(v.shape, v.dtype) for v in operands[1:]),
                pltpu.VMEM((3, 1, n_nodes), F32),
                pltpu.VMEM((9, cx + 4, cy, nz), F32),
                pltpu.VMEM((2, 6, cx, nz), F32),
                pltpu.VMEM((2, 6, cx, nz), F32),
                pltpu.VMEM((2, 6, cx, nz), F32),
                pltpu.VMEM((2, 6, cx, nz), F32),
                pltpu.VMEM((STEPS, n_dom, 3, LANES), F32),
                pltpu.VMEM((STEPS, n_dom, 3, LANES), F32),
                pltpu.VMEM((STEPS, 2, 3, SHARE), F32),
                pltpu.VMEM((STEPS, 2, 3, SHARE), F32),
                pltpu.VMEM((COLS, n_arr), BF16),
                pltpu.VMEM((n_arr, COLS), BF16),
                pltpu.VMEM((8, COLS, n_el), BF16),
                pltpu.VMEM((8, n_el, COLS), BF16),
                pltpu.VMEM((COLS, n_nodes), BF16),
                pltpu.VMEM((n_nodes, COLS), BF16),
                pltpu.VMEM((nz, n_arr), BF16),
                pltpu.VMEM((8, 8, n_el), jnp.int32),
                pltpu.VMEM((8, 8 * runs, max(n_el, n_arr)), BF16),
                pltpu.VMEM((8, 8, n_el), F32),
                pltpu.VMEM((8, 8, n_el), F32),
                pltpu.VMEM((384, n_el), BF16),
                pltpu.VMEM((192, 384), BF16),
                pltpu.VMEM((8, n_nodes), F32),
                pltpu.VMEM((8, n_nodes), F32),
                pltpu.VMEM((2 * SHARE // LANES, 8, LANES), jnp.int32),
                pltpu.VMEM((8, n_nodes), F32),
                sem,
                sem,
                sem((11,)),
                sem((2, 2, 3)),
                sem((2, 2, 3)),
                sem((2, 2)),
                sem((2, 2)),
                sem((STEPS, n_dom)),
                sem((STEPS, n_dom)),
                sem((STEPS, 2)),
                sem((STEPS, 2)),
            ],
            compiler_params=pltpu.CompilerParams(
                collective_id=0, has_side_effects=True, vmem_limit_bytes=62 * 1024 * 1024
            ),
        )(*operands)
        return basin, disp.reshape(disp_now.shape)

    spread3 = P("site", "dom", None)
    spread4 = P("site", "dom", None, None)
    slab = P(None, "dom", "site", None)
    return jax.shard_map(
        on_device,
        mesh=mesh,
        in_specs=(
            slab, slab, spread4, spread4, spread4, spread3, spread3, spread3, spread3, P(), spread4, spread4,
        ),
        out_specs=(slab, spread4),
        check_vma=False,
    )
```

time: 86.9 us -> 64.2 us (0.74)
  Pallas kernels: 75 us -> 60 us
  local copies, waits for them, and re-layouts: 10.6 us -> 3 us
    pallas_call x1, Pallas kernels: 75 us -> 60 us  [on_device(): pl.pallas_call(functools.partial(kernel, n_site, n_dom), out_shape=(jax.S...]
    unnamed x23 -> x4, local copies, waits for them, and re-layouts: 10.6 us -> 3 us
where the time goes in v2:
time: 64.2 us; the launch traced here: 63.7 us
  Pallas kernels  60 us (93%)
  local copies, waits for them, and re-layouts  3 us (5%)
  between operations  0.65 us (1%)
    pallas_call x1, Pallas kernels, on_device(): pl.pallas_call(functools.partial(kernel, n_site, n_dom), out_shape=(jax.S...  60 us
    unnamed x4, local copies, waits for them, and re-layouts  3 us

profile of v2, /device:TPU:7, one launch (start us, length us, event | category | flops | bytes accessed | tf_op | source)
XLA Modules:
  0.0 63.7 jit_solution(4626803206932100164)
XLA Ops:
  0.6 60.0 %shard_map.131 = (f32[9,8,16,256]{3,2,1,0:T(8,128)}, f32[3,1,4096]{2,1,0:T(1,128)}) custom-call(f32[9,8,16,256]{3,2,1,0:T(8,128)} %fields.1, f32[3,8,16,256]{3,2,1,0:T(8,128)} %mat_hbm.1, s32[16,128]{1,0:T(8,128)} %bitcast.19, s32[16,128]{1,0:T(8,128)} %bitcast.20, s32[8,2048]{1,0:T(8,128)} %bitcast.12, f32[1,2048]{1,0:T(1,128)} %bitcast.21, ...), custom_call_target="tpu_custom_call" | custom-call | tf_op jit(solution)/shard_map/pallas_call | solution.py:690
  60.7 0.0 copy-start
  60.7 2.4 %copy.17 = f32[9,8,16,256]{3,2,1,0:T(8,128)} copy(f32[9,8,16,256]{3,2,1,0:T(8,128)} %get-tuple-element.10) | data formatting | bytes 2359296
  63.1 0.0 copy-done
  63.1 0.6 copy.18
Async XLA Ops:
  60.7 2.4 %copy-start = (f32[3,1,4096]{2,1,0:T(1,128)S(1)}, f32[3,1,4096]{2,1,0:T(1,128)}, u32[]{:S(2)}) copy-start(f32[3,1,4096]{2,1,0:T(1,128)} %get-tuple-element.5) | copy-start | bytes 147460

commit v3 on v2

--- a/solution.py
+++ b/solution.py
@@ -272,20 +272,20 @@
         for f, kind in fields_y:
             for k in range(LOW[kind]):
                 y = cy - LOW[kind] + k
-                y_to_high[which, at, pl.ds(x, 1), :] = planes[f][y : y + 1]
+                y_to_high[which, at, x : x + 1, :] = planes[f][y : y + 1]
                 at += 1
         at = 0
         for f, kind in fields_y:
             for k in range(HIGH[kind]):
-                y_to_low[which, at, pl.ds(x, 1), :] = planes[f][k : k + 1]
+                y_to_low[which, at, x : x + 1, :] = planes[f][k : k + 1]
                 at += 1
 
     def y_edges(which, fields_y, x):
         edges = {}
         low_at = high_at = 0
         for f, kind in fields_y:
-            low = [y_low[which, low_at + k, pl.ds(x, 1), :] for k in range(LOW[kind])]
-            high = [y_high[which, high_at + k, pl.ds(x, 1), :] for k in range(HIGH[kind])]
+            low = [y_low[which, low_at + k, x : x + 1, :] for k in range(LOW[kind])]
+            high = [y_high[which, high_at + k, x : x + 1, :] for k in range(HIGH[kind])]
             low_at += LOW[kind]
             high_at += HIGH[kind]
             edges[f] = (low, high)
@@ -305,7 +305,7 @@
         return diff_rolled(kind, st[f, x + 2], 1, lane_iota, (0.0, 0.0), (0.0, 0.0))
 
     def velocity_half():
-        def body(x, carry):
+        def body(x):
             edges = y_edges(0, STRESS_Y, x)
             b = DT * mat[0, x]
             planes = {
@@ -319,12 +319,12 @@
             for f, plane in planes.items():
                 st[f, x + 2] = plane
             y_pack(1, VEL_Y, x, planes)
-            return carry
-
-        lax.fori_loop(0, cx, body, 0)
+
+        for x in range(cx):
+            body(x)
 
     def stress_half():
-        def body(x, carry):
+        def body(x):
             edges = y_edges(1, VEL_Y, x)
             lam, mu = mat[1, x], mat[2, x]
             exx = diff_x("B", 0, x)
@@ -343,9 +343,9 @@
             for f, plane in planes.items():
                 st[f, x + 2] = plane
             y_pack(0, STRESS_Y, x, planes)
-            return carry
-
-        lax.fori_loop(0, cx, body, 0)
+
+        for x in range(cx):
+            body(x)
 
     def sample(k):
         n = n_arr // 2
@@ -379,15 +379,12 @@
         )
 
     def sample_start(k):
-        def body(d, carry):
+        for d in range(1, n_dom):
             sample_copy(k, d).start()
-            return carry
-
-        lax.fori_loop(1, n_dom, body, 0)
         samp_recv[k, me_d] = samp_send[k, me_d]
 
     def sample_wait(k):
-        def body(d, carry):
+        for d in range(1, n_dom):
             here = lax.rem(me_d + n_dom - d, n_dom)
             copy = pltpu.make_async_remote_copy(
                 src_ref=samp_send.at[k, here],
@@ -399,9 +396,6 @@
             )
             copy.wait_recv()
             sample_copy(k, d).wait_send()
-            return carry
-
-        lax.fori_loop(1, n_dom, body, 0)
 
     def run(h):
         return pl.ds(h * COLS, COLS)
@@ -486,7 +480,7 @@
 
     def prep_hot():
         for j in range(8):
-            one_hot_both(elem[j : j + 1] & (COLS - 1), oh_elem.at[j], oh_elem_t.at[j])
+            one_hot_both(elem[j : j + 1] & (COLS - 1), oh_elem.at[j], oh_elem_t.at[pl.ds(j * n_el, n_el)])
             high_rows[j] = jnp.broadcast_to(elem[j : j + 1] >> 8, (8, n_el))
 
     def prep_cell():
@@ -516,9 +510,9 @@
             got = samp_recv[k, p]
             top, rest = split(got)
             values = jnp.concatenate([rest, top, jnp.ones((2, LANES), F32)], axis=0)
-            spread(recv_node[p : p + 1] >> 8, values, lhs.at[0, :, pl.ds(p * LANES, LANES)])
+            spread(recv_node[p : p + 1] >> 8, values, lhs.at[:, pl.ds(p * LANES, LANES)])
         placed = by_node(
-            jnp.dot(lhs[0, :, pl.ds(0, n_arr)], oh_recv_t[...], preferred_element_type=F32)
+            jnp.dot(lhs[:, pl.ds(0, n_arr)], oh_recv_t[...], preferred_element_type=F32)
         )
         old, row = node[...], sub(node.shape)
         both = placed + pltpu.roll(placed, 3, 0)
@@ -569,14 +563,10 @@
                     + inn[j, :, at] * response[128 + 8 * j : 136 + 8 * j]
                 )
                 top, rest = split(value)
-                spread(elem[j : j + 1, at] >> 8, jnp.where(first, top, rest), lhs.at[j, :, at])
+                spread(elem[j : j + 1, at] >> 8, jnp.where(first, top, rest), lhs.at[:, pl.ds(j * n_el + i * wide, wide)])
 
     def element_add():
-        total = jnp.zeros((8 * runs, COLS), F32)
-        for j in range(8):
-            total = total + jnp.dot(
-                lhs[j, :, pl.ds(0, n_el)], oh_elem_t[j], preferred_element_type=F32
-            )
+        total = jnp.dot(lhs[...], oh_elem_t[...], preferred_element_type=F32)
         both = by_node(total)
         force[...] = both + pltpu.roll(both, 5, 0)
 
@@ -623,30 +613,30 @@
             prev[:, at] = u
             node[:, at] = jnp.where(sub(u.shape) < 3, following, u)
 
-    def first_pack(x, carry):
+    for x in range(cx):
         y_pack(0, STRESS_Y, x, {f: st[f, x + 2] for f, _ in STRESS_Y})
-        return carry
-
-    lax.fori_loop(0, cx, first_pack, 0)
     expected = (
         n_dom - 1 + jnp.where(me_s > 0, 1, 0) + jnp.where(me_s < n_site - 1, 1, 0)
     ).astype(jnp.int32)
     pl.semaphore_wait(barrier, expected)
     halo_start(0, STRESS_X, STRESS_Y)
+    prep_cell()
     prep_nodes()
     prep_k()
     prep_arr()
-    prep_hot()
     prep_slot()
-    prep_cell()
     for k in range(STEPS):
         halo_wait(0, STRESS_X, STRESS_Y)
         velocity_half()
         halo_start(1, VEL_X, VEL_Y)
         sample(k)
         sample_start(k)
-        if k:
-            rim_finish(k - 1)
+        if k == 0:
+            prep_hot()
+        else:
+            element_response()
+            element_add()
+            rim_start(k - 1)
         halo_wait(1, VEL_X, VEL_Y)
         stress_half()
         if k < STEPS - 1:
@@ -655,11 +645,13 @@
             store = pltpu.make_async_copy(st.at[:, pl.ds(2, cx)], basin_out, out_sem)
             store.start()
         sample_wait(k)
+        if k:
+            rim_finish(k - 1)
         place(k)
         element_cols(k)
-        element_response()
-        element_add()
-        rim_start(k)
+    element_response()
+    element_add()
+    rim_start(STEPS - 1)
     rim_finish(STEPS - 1)
     for c in range(3):
         disp_v[c] = node[c : c + 1, :]
@@ -667,6 +659,22 @@
     disp_store.start()
     disp_store.wait()
     store.wait()
+
+
+def hand_over(basin_in, disp_in, basin_out, disp_out, basin, disp, load_sems, store_sems):
+    loads = [pltpu.make_async_copy(basin_in.at[f], basin.at[f], load_sems.at[f]) for f in range(9)]
+    loads.append(pltpu.make_async_copy(disp_in, disp, load_sems.at[9]))
+    stores = [
+        pltpu.make_async_copy(basin.at[f], basin_out.at[f], store_sems.at[f]) for f in range(9)
+    ]
+    stores.append(pltpu.make_async_copy(disp, disp_out, store_sems.at[9]))
+    for copy in loads:
+        copy.start()
+    for load, store in zip(loads, stores):
+        load.wait()
+        store.start()
+    for copy in stores:
+        copy.wait()
 
 
 def solution(mesh):
@@ -687,12 +695,13 @@
             fields, material, send_cell[0, 0], recv_node[0, 0], elements[0, 0], modulus[0], node_mass[0], outer_flag[0],
             shared_slot[0], stiffness, disp_now.reshape(3, 1, n_nodes), disp_prev.reshape(3, 1, n_nodes),
         )
+        shapes = (
+            jax.ShapeDtypeStruct(fields.shape, F32),
+            jax.ShapeDtypeStruct((3, 1, n_nodes), F32),
+        )
         basin, disp = pl.pallas_call(
             functools.partial(kernel, n_site, n_dom),
-            out_shape=(
-                jax.ShapeDtypeStruct(fields.shape, F32),
-                jax.ShapeDtypeStruct((3, 1, n_nodes), F32),
-            ),
+            out_shape=shapes,
             in_specs=[hbm] * 12,
             out_specs=(hbm, hbm),
             scratch_shapes=[
@@ -710,12 +719,12 @@
                 pltpu.VMEM((COLS, n_arr), BF16),
                 pltpu.VMEM((n_arr, COLS), BF16),
                 pltpu.VMEM((8, COLS, n_el), BF16),
-                pltpu.VMEM((8, n_el, COLS), BF16),
+                pltpu.VMEM((8 * n_el, COLS), BF16),
                 pltpu.VMEM((COLS, n_nodes), BF16),
                 pltpu.VMEM((n_nodes, COLS), BF16),
                 pltpu.VMEM((nz, n_arr), BF16),
                 pltpu.VMEM((8, 8, n_el), jnp.int32),
-                pltpu.VMEM((8, 8 * runs, max(n_el, n_arr)), BF16),
+                pltpu.VMEM((8 * runs, 8 * n_el), BF16),
                 pltpu.VMEM((8, 8, n_el), F32),
                 pltpu.VMEM((8, 8, n_el), F32),
                 pltpu.VMEM((384, n_el), BF16),
@@ -740,6 +749,19 @@
                 collective_id=0, has_side_effects=True, vmem_limit_bytes=62 * 1024 * 1024
             ),
         )(*operands)
+        basin, disp = pl.pallas_call(
+            hand_over,
+            out_shape=shapes,
+            in_specs=[hbm] * 2,
+            out_specs=(hbm, hbm),
+            scratch_shapes=[
+                pltpu.VMEM(fields.shape, F32),
+                pltpu.VMEM((3, 1, n_nodes), F32),
+                sem((10,)),
+                sem((10,)),
+            ],
+            compiler_params=pltpu.CompilerParams(vmem_limit_bytes=62 * 1024 * 1024),
+        )(basin, disp)
         return basin, disp.reshape(disp_now.shape)
 
     spread3 = P("site", "dom", None)

time: 64.2 us -> 60.3 us (0.939)
  local copies, waits for them, and re-layouts: 3 us -> 0 us
  Pallas kernels: 60 us -> 58.8 us
    unnamed x4 -> x0, local copies, waits for them, and re-layouts: 3 us -> none
    pallas_call x1 -> x2, Pallas kernels: 60 us -> 58.8 us  [the longest x1 56.7 us: on_device(): pl.pallas_call(functools.partial(kernel, n_site, n_dom), out_shape=shapes...]
where the time goes in v3:
time: 60.3 us; the launch traced here: 59.7 us
  Pallas kernels  58.8 us (98%)
  between operations  0.82 us (1%)
    pallas_call x1, Pallas kernels, on_device(): pl.pallas_call(functools.partial(kernel, n_site, n_dom), out_shape=shapes...  56.7 us
    pallas_call x1, Pallas kernels, on_device(): pl.pallas_call(hand_over, out_shape=shapes, in_specs=[hbm] * 2, out_specs...  2.17 us

profile of v3, /device:TPU:7, one launch (start us, length us, event | category | flops | bytes accessed | tf_op | source)
XLA Modules:
  0.0 59.7 jit_solution(9368466555372071127)
XLA Ops:
  0.6 56.7 %shard_map.131 = (f32[9,8,16,256]{3,2,1,0:T(8,128)}, f32[3,1,4096]{2,1,0:T(1,128)}) custom-call(f32[9,8,16,256]{3,2,1,0:T(8,128)} %fields.1, f32[3,8,16,256]{3,2,1,0:T(8,128)} %mat_hbm.1, s32[16,128]{1,0:T(8,128)} %bitcast.18, s32[16,128]{1,0:T(8,128)} %bitcast.19, s32[8,2048]{1,0:T(8,128)} %bitcast.12, f32[1,2048]{1,0:T(1,128)} %bitcast.20, ...), custom_call_target="tpu_custom_call" | custom-call | tf_op jit(solution)/shard_map/pallas_call | solution.py:702
  57.3 2.2 %shard_map.132 = (f32[9,8,16,256]{3,2,1,0:T(8,128)}, f32[3,1,4096]{2,1,0:T(1,128)}) custom-call(f32[9,8,16,256]{3,2,1,0:T(8,128)} %get-tuple-element.6.basin_in, f32[3,1,4096]{2,1,0:T(1,128)} %get-tuple-element.7.disp_in), custom_call_target="tpu_custom_call" | custom-call | tf_op jit(solution)/shard_map/pallas_call | solution.py:752

commit v4 on v3

--- a/solution.py
+++ b/solution.py
@@ -234,13 +234,16 @@
         "y": (me_s > 0, me_s < n_site - 1),
     }
 
-    def halo_start(which, fields_x, fields_y):
+    def halo_start_x(which, fields_x):
         for upward in (False, True):
 
             @pl.when(has["x"][upward])
             def _():
                 for copy in x_copies(which, fields_x, upward):
                     copy.start()
+
+    def halo_start_y(which, fields_y):
+        for upward in (False, True):
 
             @pl.when(has["y"][upward])
             def _():
@@ -303,6 +306,8 @@
 
     def diff_z(kind, f, x):
         return diff_rolled(kind, st[f, x + 2], 1, lane_iota, (0.0, 0.0), (0.0, 0.0))
+
+    ends = (0, 1, cx - 2, cx - 1)
 
     def velocity_half():
         def body(x):
@@ -320,10 +325,14 @@
                 st[f, x + 2] = plane
             y_pack(1, VEL_Y, x, planes)
 
-        for x in range(cx):
+        for x in ends:
             body(x)
-
-    def stress_half():
+        halo_start_x(1, VEL_X)
+        for x in range(2, cx - 2):
+            body(x)
+        halo_start_y(1, VEL_Y)
+
+    def stress_half(last):
         def body(x):
             edges = y_edges(1, VEL_Y, x)
             lam, mu = mat[1, x], mat[2, x]
@@ -344,8 +353,14 @@
                 st[f, x + 2] = plane
             y_pack(0, STRESS_Y, x, planes)
 
-        for x in range(cx):
+        for x in ends:
             body(x)
+        if not last:
+            halo_start_x(0, STRESS_X)
+        for x in range(2, cx - 2):
+            body(x)
+        if not last:
+            halo_start_y(0, STRESS_Y)
 
     def sample(k):
         n = n_arr // 2
@@ -619,7 +634,8 @@
         n_dom - 1 + jnp.where(me_s > 0, 1, 0) + jnp.where(me_s < n_site - 1, 1, 0)
     ).astype(jnp.int32)
     pl.semaphore_wait(barrier, expected)
-    halo_start(0, STRESS_X, STRESS_Y)
+    halo_start_x(0, STRESS_X)
+    halo_start_y(0, STRESS_Y)
     prep_cell()
     prep_nodes()
     prep_k()
@@ -628,7 +644,6 @@
     for k in range(STEPS):
         halo_wait(0, STRESS_X, STRESS_Y)
         velocity_half()
-        halo_start(1, VEL_X, VEL_Y)
         sample(k)
         sample_start(k)
         if k == 0:
@@ -638,10 +653,8 @@
             element_add()
             rim_start(k - 1)
         halo_wait(1, VEL_X, VEL_Y)
-        stress_half()
-        if k < STEPS - 1:
-            halo_start(0, STRESS_X, STRESS_Y)
-        else:
+        stress_half(k == STEPS - 1)
+        if k == STEPS - 1:
             store = pltpu.make_async_copy(st.at[:, pl.ds(2, cx)], basin_out, out_sem)
             store.start()
         sample_wait(k)

time: 60.3 us -> 58.1 us (0.964)
  Pallas kernels: 58.8 us -> 57.1 us
    pallas_call x1, Pallas kernels: 56.7 us -> 55 us  [on_device(): pl.pallas_call(functools.partial(kernel, n_site, n_dom), out_shape=shapes...]
where the time goes in v4:
time: 58.1 us; the launch traced here: 58 us
  Pallas kernels  57.1 us (98%)
  between operations  0.82 us (1%)
    pallas_call x1, Pallas kernels, on_device(): pl.pallas_call(functools.partial(kernel, n_site, n_dom), out_shape=shapes...  55 us
    pallas_call x1, Pallas kernels, on_device(): pl.pallas_call(hand_over, out_shape=shapes, in_specs=[hbm] * 2, out_specs...  2.17 us

profile of v4, /device:TPU:7, one launch (start us, length us, event | category | flops | bytes accessed | tf_op | source)
XLA Modules:
  0.0 58.0 jit_solution(9387054355533964672)
XLA Ops:
  0.6 55.0 %shard_map.131 = (f32[9,8,16,256]{3,2,1,0:T(8,128)}, f32[3,1,4096]{2,1,0:T(1,128)}) custom-call(f32[9,8,16,256]{3,2,1,0:T(8,128)} %fields.1, f32[3,8,16,256]{3,2,1,0:T(8,128)} %mat_hbm.1, s32[16,128]{1,0:T(8,128)} %bitcast.18, s32[16,128]{1,0:T(8,128)} %bitcast.19, s32[8,2048]{1,0:T(8,128)} %bitcast.12, f32[1,2048]{1,0:T(1,128)} %bitcast.20, ...), custom_call_target="tpu_custom_call" | custom-call | tf_op jit(solution)/shard_map/pallas_call | solution.py:715
  55.6 2.2 %shard_map.132 = (f32[9,8,16,256]{3,2,1,0:T(8,128)}, f32[3,1,4096]{2,1,0:T(1,128)}) custom-call(f32[9,8,16,256]{3,2,1,0:T(8,128)} %get-tuple-element.6.basin_in, f32[3,1,4096]{2,1,0:T(1,128)} %get-tuple-element.7.disp_in), custom_call_target="tpu_custom_call" | custom-call | tf_op jit(solution)/shard_map/pallas_call | solution.py:765
